TPU v7x, 32 devices: a whole 2x2x4 slice. The times are simulated.
32 devices in a mesh: dp: 16 (over z, y, core), expert: 2 (over x).
Axes of the slice: x: 2, y: 2, z: 4, core: 2. Of those that a mesh axis runs over, the one named last changes fastest.
Arguments:
- tokens: bfloat16 [6144, 2048], P(('dp', 'expert')), may hold values from -6 to 6
- routes: int32 [6144, 6], P(('dp', 'expert')), may hold values from 0 to 63, as said below
- gate_scale: float32 [6144, 6], P(('dp', 'expert')), may hold values from 0.2 to 2
- w_gate: bfloat16 [2, 2048, 768], P('expert', 'dp'), may hold values from -0.125 to 0.125
- w_up: bfloat16 [2, 2048, 768], P('expert', 'dp'), may hold values from -0.125 to 0.125
- w_down: bfloat16 [2, 2048, 768], P('expert', 'dp'), may hold values from -0.21875 to 0.21875
- d_out: bfloat16 [6144, 2048], P(('dp', 'expert')), may hold values from -6 to 6
Outputs:
- layer_out: bfloat16 [6144, 2048], P(('dp', 'expert'))
- d_tokens: bfloat16 [6144, 2048], P(('dp', 'expert'))
- grad_gate: float32 [2, 2048, 768], P('expert', 'dp')
- grad_up: float32 [2, 2048, 768], P('expert', 'dp')
- grad_down: float32 [2, 2048, 768], P('expert', 'dp')
Inputs may be any that keep to these rules, and one draw needn't show every extreme that they name: `routes`: each token names 6 different experts. The experts of this window are 0 to 1; among the 192 tokens of one device no window expert is named by more than 32 tokens.
All inputs are finite; a program needn't handle non-finite values.
Results may differ from a plain program's by a relative error of at most 0.02.
Values may be sent and summed in bfloat16 or wider, within the bound.
No kernel may reach another device: no remote copies, remote signals or barrier semaphores. Data moves between devices by JAX's collectives and lax.ppermute only.
A program may use at most 64 MiB of HBM per device.

v0:
```python
import jax
import jax.numpy as jnp
from jax import lax
from jax.sharding import PartitionSpec as P

CAP = 32


def shards(tokens, routes, gate_scale, w_gate, w_up, w_down, d_out):
    experts_here = lax.axis_size("expert")
    tok_count = tokens.shape[0]
    width = tokens.shape[1]
    choices_per = routes.shape[1]
    capacity = CAP
    slots = experts_here * capacity
    flat_count = tok_count * choices_per
    combine = gate_scale / jnp.sum(gate_scale, axis=1, keepdims=True)
    flat_ids = routes.reshape(flat_count)
    flat_weight = combine.reshape(flat_count)
    live = flat_ids < experts_here
    onehot = (
        (flat_ids[:, None] == jnp.arange(experts_here, dtype=jnp.int32)[None, :]) & live[:, None]
    ).astype(jnp.int32)
    position = jnp.sum((jnp.cumsum(onehot, axis=0) - onehot) * onehot, axis=1)
    dest = jnp.where(live, flat_ids * capacity + position, slots)
    match = jnp.arange(slots, dtype=jnp.int32)[:, None] == dest[None, :]
    filled = jnp.any(match, axis=1)
    owner = jnp.sum(
        jnp.where(match, (jnp.arange(flat_count, dtype=jnp.int32) // choices_per)[None, :], 0),
        axis=1,
    )
    slot_weight = jnp.sum(jnp.where(match, flat_weight[None, :], 0.0), axis=1)
    send_x = jnp.where(filled[:, None], tokens[owner], jnp.zeros((), jnp.bfloat16))
    send_d = jnp.where(
        filled[:, None], d_out[owner].astype(jnp.float32) * slot_weight[:, None], 0.0
    ).astype(jnp.bfloat16)
    send_x = send_x.reshape(experts_here, capacity, width)
    send_d = send_d.reshape(experts_here, capacity, width)
    full_gate, full_up, full_down = (
        lax.all_gather(w_gate, "dp", axis=1, tiled=True),
        lax.all_gather(w_up, "dp", axis=1, tiled=True),
        lax.all_gather(w_down, "dp", axis=1, tiled=True),
    )
    recv_x, recv_d = (
        lax.all_to_all(send_x, "expert", split_axis=0, concat_axis=0, tiled=True),
        lax.all_to_all(send_d, "expert", split_axis=0, concat_axis=0, tiled=True),
    )
    weight_gate = full_gate[0]
    weight_up = full_up[0]
    weight_down = full_down[0]
    rows_x = recv_x.reshape(slots, width)
    rows_d = recv_d.reshape(slots, width)
    contract_last = (((1,), (1,)), ((), ()))
    contract_first = (((0,), (0,)), ((), ()))
    gate = jnp.dot(rows_x, weight_gate, preferred_element_type=jnp.float32)
    up = jnp.dot(rows_x, weight_up, preferred_element_type=jnp.float32)
    sig = jax.nn.sigmoid(gate)
    act = gate * sig
    hidden = (act * up).astype(jnp.bfloat16)
    expert_out = lax.dot_general(
        hidden, weight_down, contract_last, preferred_element_type=jnp.float32
    ).astype(jnp.bfloat16)
    d_hidden = jnp.dot(rows_d, weight_down, preferred_element_type=jnp.float32)
    d_gate = (d_hidden * up * sig * (1.0 + gate * (1.0 - sig))).astype(jnp.bfloat16)
    d_up = (d_hidden * act).astype(jnp.bfloat16)
    d_in = (
        lax.dot_general(d_gate, weight_gate, contract_last, preferred_element_type=jnp.float32)
        + lax.dot_general(d_up, weight_up, contract_last, preferred_element_type=jnp.float32)
    ).astype(jnp.bfloat16)
    back_out, back_in = (
        lax.all_to_all(
            expert_out.reshape(experts_here, capacity, width),
            "expert",
            split_axis=0,
            concat_axis=0,
            tiled=True,
        ),
        lax.all_to_all(
            d_in.reshape(experts_here, capacity, width),
            "expert",
            split_axis=0,
            concat_axis=0,
            tiled=True,
        ),
    )
    term_gate = lax.dot_general(rows_x, d_gate, contract_first, preferred_element_type=jnp.float32)
    term_up = lax.dot_general(rows_x, d_up, contract_first, preferred_element_type=jnp.float32)
    term_down = lax.dot_general(rows_d, hidden, contract_first, preferred_element_type=jnp.float32)
    grad_gate, grad_up, grad_down = (
        lax.psum_scatter(
            term_gate.astype(jnp.bfloat16), "dp", scatter_dimension=0, tiled=True
        ).astype(jnp.float32),
        lax.psum_scatter(
            term_up.astype(jnp.bfloat16), "dp", scatter_dimension=0, tiled=True
        ).astype(jnp.float32),
        lax.psum_scatter(
            term_down.astype(jnp.bfloat16), "dp", scatter_dimension=0, tiled=True
        ).astype(jnp.float32),
    )
    back_out = back_out.reshape(slots, width)
    back_in = back_in.reshape(slots, width)
    dest_tok = dest.reshape(tok_count, choices_per)
    live_tok = live.reshape(tok_count, choices_per)
    weight_tok = jnp.where(live_tok, combine, 0.0)
    safe_rows = jnp.where(live_tok, dest_tok, 0)
    total_out = jnp.zeros((tok_count, width), jnp.float32)
    total_in = jnp.zeros((tok_count, width), jnp.float32)
    for choice_index in range(choices_per):
        rows_pick = safe_rows[:, choice_index]
        total_out = total_out + weight_tok[:, choice_index : choice_index + 1] * back_out[
            rows_pick
        ].astype(jnp.float32)
        total_in = total_in + jnp.where(
            live_tok[:, choice_index : choice_index + 1],
            back_in[rows_pick].astype(jnp.float32),
            0.0,
        )
    layer_out = total_out.astype(jnp.bfloat16)
    d_tokens = total_in.astype(jnp.bfloat16)
    return (layer_out, d_tokens, grad_gate[None], grad_up[None], grad_down[None])


def solution(mesh):
    placed = (
        P(("dp", "expert"), None),
        P(("dp", "expert"), None),
        P(("dp", "expert"), None),
        P("expert", "dp", None),
        P("expert", "dp", None),
        P("expert", "dp", None),
        P(("dp", "expert"), None),
    )
    return jax.shard_map(
        shards,
        mesh=mesh,
        in_specs=placed,
        out_specs=(
            P(("dp", "expert"), None),
            P(("dp", "expert"), None),
            P("expert", "dp", None),
            P("expert", "dp", None),
            P("expert", "dp", None),
        ),
        check_vma=False,
    )
```

profile of v0, /device:TPU:0, one launch (start us, length us, event | category | flops | bytes accessed | tf_op | source)
XLA Modules:
  0.0 367.9 jit_solution(6330250649687845058)
XLA Ops:
  15.5 4.2 %all-to-all-start.2 = ((bf16[2,32,2048]{2,1,0:T(8,128)(2,1)}), bf16[2,32,2048]{2,1,0:T(8,128)(2,1)S(1)}, u32[]{:S(2)}, u32[]{:S(2)}) async-start(bf16[2,32,2048]{2,1,0:T(8,128)(2,1)} %fusion.22), calls=%async_computation.2 | async-start | bytes 524288 | tf_op jit(solution)/shard_map/all_to_all | solution.py:46
  21.3 4.3 %all-to-all-done.2 = bf16[2,32,2048]{2,1,0:T(8,128)(2,1)S(1)} async-done(((bf16[2,32,2048]{2,1,0:T(8,128)(2,1)}), bf16[2,32,2048]{2,1,0:T(8,128)(2,1)S(1)}, u32[]{:S(2)}, u32[]{:S(2)}) %all-to-all-start.2) | async-done | bytes 262176 | tf_op jit(solution)/shard_map/all_to_all | solution.py:46
  25.6 3.4 all-to-all-start
  29.1 29.3 %all-gather.8.cloned.1.call-done = bf16[1,2048,768]{2,1,0:T(8,128)(2,1)} async-done(((bf16[1,128,768]{2,1,0:T(8,128)(2,1)}), bf16[1,2048,768]{2,1,0:T(8,128)(2,1)}) %all-gather.8.cloned.1.call-update) | async-done | bytes 3145744 | tf_op jit(solution)/shard_map/all_gather | solution.py:42
  58.4 2.5 fusion
  61.0 43.8 %all-gather.6.cloned.1.call-done = bf16[1,2048,768]{2,1,0:T(8,128)(2,1)} async-done(((bf16[1,128,768]{2,1,0:T(8,128)(2,1)}), bf16[1,2048,768]{2,1,0:T(8,128)(2,1)}) %all-gather.6.cloned.1.call-update) | async-done | bytes 3145744 | tf_op jit(solution)/shard_map/all_gather | solution.py:41
  104.8 2.5 fusion.6
  107.3 43.8 %all-gather.4.cloned.1.call-done = bf16[1,2048,768]{2,1,0:T(8,128)(2,1)} async-done(((bf16[1,128,768]{2,1,0:T(8,128)(2,1)}), bf16[1,2048,768]{2,1,0:T(8,128)(2,1)}) %all-gather.4.cloned.1.call-update) | async-done | bytes 3145744 | tf_op jit(solution)/shard_map/all_gather | solution.py:40
  151.1 2.6 multiply_convert_fusion.1
  153.7 2.7 convolution_convert_fusion
  156.5 2.7 convolution_convert_fusion.2
  159.3 2.7 convolution_convert_fusion.1
  162.8 3.2 fusion.4
  167.8 3.4 all-to-all-start.3
  171.2 3.8 %fusion.18 = bf16[64,2048]{1,0:T(8,128)(2,1)} fusion(bf16[64,768]{1,0:T(8,128)(2,1)S(1)} %get-tuple-element.16, bf16[1,2048,768]{2,1,0:T(8,128)(2,1)} %all-gather.8.cloned.1.call-done), kind=kOutput, calls=%fused_computation.31 | convolution fusion | flops 201457664 | bytes 3506176 | tf_op jit(solution)/shard_map/dot_general | solution.py:60
  175.0 2.1 all-to-all-done.3
  177.1 3.6 all-to-all-start.1
  182.8 2.9 all-to-all-done.1
  190.1 2.1 gather_fusion.11
  200.2 2.1 gather_fusion.1
  206.4 4.5 %add_convert_fusion = bf16[192,2048]{1,0:T(8,128)(2,1)} fusion(bf16[192,2048]{1,0:T(8,128)(2,1)} %gather_fusion.13, bf16[192,2048]{1,0:T(8,128)(2,1)} %gather_fusion.12, bf16[192,2048]{1,0:T(8,128)(2,1)} %gather_fusion.11, bf16[192,2048]{1,0:T(8,128)(2,1)} %gather_fusion.10, bf16[192,2048]{1,0:T(8,128)(2,1)} %gather_fusion.9, ...), kind=kLoop, calls=%fused_computation.32 | loop fusion | flops 7077888 | bytes 5506176 | tf_op jit(solution)/shard_map/convert_element_type | solution.py:119
  212.7 8.9 %reduce-scatter.8.cloned.1.call-done = bf16[128,768]{1,0:T(8,128)(2,1)} async-done(((bf16[2048,768]{1,0:T(8,128)(2,1)}), bf16[128,768]{1,0:T(8,128)(2,1)}) %reduce-scatter.8.cloned.1.call-update) | async-done | bytes 196624 | tf_op jit(solution)/shard_map/reduce_scatter | solution.py:96
  223.3 67.2 %reduce-scatter.4.cloned.1.call-done = bf16[128,768]{1,0:T(8,128)(2,1)} async-done(((bf16[2048,768]{1,0:T(8,128)(2,1)}), bf16[128,768]{1,0:T(8,128)(2,1)}) %reduce-scatter.4.cloned.1.call-update) | async-done | bytes 196624 | tf_op jit(solution)/shard_map/reduce_scatter | solution.py:90
  292.2 67.2 %reduce-scatter.6.cloned.1.call-done = bf16[128,768]{1,0:T(8,128)(2,1)} async-done(((bf16[2048,768]{1,0:T(8,128)(2,1)}), bf16[128,768]{1,0:T(8,128)(2,1)}) %reduce-scatter.6.cloned.1.call-update) | async-done | bytes 196624 | tf_op jit(solution)/shard_map/reduce_scatter | solution.py:93
  (83 shorter events, 38.0 us)
Async XLA Ops:
  7.2 6.8 %copy-start = (bf16[192,2048]{1,0:T(8,128)(2,1)S(1)}, bf16[192,2048]{1,0:T(8,128)(2,1)}, u32[]{:S(2)}) copy-start(bf16[192,2048]{1,0:T(8,128)(2,1)} %param.13) | copy-start | bytes 2359300
  7.2 51.3 %all-gather.8.cloned.1.call-start = ((), (), s32[]{:S(2)}) async-start(), calls=%async_computation.9 | async-start | bytes 3342336 | tf_op jit(solution)/shard_map/all_gather | solution.py:42
  7.9 96.9 %all-gather.6.cloned.1.call-start = ((), (), s32[]{:S(2)}) async-start(), calls=%async_computation.8 | async-start | bytes 3342336 | tf_op jit(solution)/shard_map/all_gather | solution.py:41
  8.7 142.4 %all-gather.4.cloned.1.call-start = ((), (), s32[]{:S(2)}) async-start(), calls=%async_computation.7 | async-start | bytes 3342336 | tf_op jit(solution)/shard_map/all_gather | solution.py:40
  13.9 5.8 %copy-start.2 = (bf16[192,2048]{1,0:T(8,128)(2,1)S(1)}, bf16[192,2048]{1,0:T(8,128)(2,1)}, u32[]{:S(2)}) copy-start(bf16[192,2048]{1,0:T(8,128)(2,1)} %param.7) | copy-start | bytes 2359300
  15.5 10.1 %all-to-all-start.2 = ((bf16[2,32,2048]{2,1,0:T(8,128)(2,1)}), bf16[2,32,2048]{2,1,0:T(8,128)(2,1)S(1)}, u32[]{:S(2)}, u32[]{:S(2)}) async-start(bf16[2,32,2048]{2,1,0:T(8,128)(2,1)} %fusion.22), calls=%async_computation.2 | async-start | bytes 524288 | tf_op jit(solution)/shard_map/all_to_all | solution.py:46
  25.6 35.4 %all-to-all-start = ((bf16[2,32,2048]{2,1,0:T(8,128)(2,1)}), bf16[2,32,2048]{2,1,0:T(8,128)(2,1)S(1)}, u32[]{:S(2)}, u32[]{:S(2)}) async-start(bf16[2,32,2048]{2,1,0:T(8,128)(2,1)} %broadcast_select_fusion), calls=%async_computation | async-start | bytes 524288 | tf_op jit(solution)/shard_map/all_to_all | solution.py:45
  29.1 192.6 %reduce-scatter.8.cloned.1.call-start = ((), (), s32[]{:S(2)}) async-start(), calls=%async_computation.12 | async-start | bytes 3342336 | tf_op jit(solution)/shard_map/reduce_scatter | solution.py:96
  156.4 134.1 %reduce-scatter.4.cloned.1.call-start = ((), (), s32[]{:S(2)}) async-start(), calls=%async_computation.10 | async-start | bytes 3342336 | tf_op jit(solution)/shard_map/reduce_scatter | solution.py:90
  159.2 200.2 %reduce-scatter.6.cloned.1.call-start = ((), (), s32[]{:S(2)}) async-start(), calls=%async_computation.11 | async-start | bytes 3342336 | tf_op jit(solution)/shard_map/reduce_scatter | solution.py:93
  162.0 0.7 copy-start.7
  162.8 3.2 copy-start.1
  167.8 9.3 %all-to-all-start.3 = ((bf16[2,32,2048]{2,1,0:T(8,128)(2,1)}), bf16[2,32,2048]{2,1,0:T(8,128)(2,1)S(1)}, u32[]{:S(2)}, u32[]{:S(2)}) async-start(bf16[2,32,2048]{2,1,0:T(8,128)(2,1)} %bitcast.24), calls=%async_computation.3 | async-start | bytes 524288 | tf_op jit(solution)/shard_map/all_to_all | solution.py:78
  177.1 8.6 %all-to-all-start.1 = ((bf16[2,32,2048]{2,1,0:T(8,128)(2,1)}), bf16[2,32,2048]{2,1,0:T(8,128)(2,1)S(1)}, u32[]{:S(2)}, u32[]{:S(2)}) async-start(bf16[2,32,2048]{2,1,0:T(8,128)(2,1)} %bitcast.9), calls=%async_computation.1 | async-start | bytes 524288 | tf_op jit(solution)/shard_map/all_to_all | solution.py:71
  206.4 4.5 %copy-start.3 = (bf16[192,2048]{1,0:T(8,128)(2,1)S(1)}, bf16[192,2048]{1,0:T(8,128)(2,1)}, u32[]{:S(2)}) copy-start(bf16[192,2048]{1,0:T(8,128)(2,1)} %gather_fusion.4) | copy-start | bytes 2359300
  206.4 4.5 %copy-start.4 = (bf16[192,2048]{1,0:T(8,128)(2,1)S(1)}, bf16[192,2048]{1,0:T(8,128)(2,1)}, u32[]{:S(2)}) copy-start(bf16[192,2048]{1,0:T(8,128)(2,1)} %gather_fusion.3) | copy-start | bytes 2359300
  206.4 4.5 %copy-start.5 = (bf16[192,2048]{1,0:T(8,128)(2,1)S(1)}, bf16[192,2048]{1,0:T(8,128)(2,1)}, u32[]{:S(2)}) copy-start(bf16[192,2048]{1,0:T(8,128)(2,1)} %gather_fusion.1) | copy-start | bytes 2359300
  206.4 4.5 %copy-start.6 = (bf16[192,2048]{1,0:T(8,128)(2,1)S(1)}, bf16[192,2048]{1,0:T(8,128)(2,1)}, u32[]{:S(2)}) copy-start(bf16[192,2048]{1,0:T(8,128)(2,1)} %gather_fusion.2) | copy-start | bytes 2359300
Sparse Core Ops, SparseCore 0:
  10.3 48.1 all-gather.7
  60.7 43.9 all-gather.5
  107.1 43.9 all-gather.3
  156.6 65.0 reduce-scatter.7
  225.3 65.2 reduce-scatter.3
  294.2 65.1 reduce-scatter.5
where the time goes:
time: 369 us; the launch traced here: 368 us
  waiting for transfers between devices  272 us (74%)
  local copies, waits for them, and re-layouts  26.6 us (7%)
  matrix products  24.5 us (7%)
  other arithmetic  15.9 us (4%)
  starting transfers between devices  15 us (4%)
  between operations  14.4 us (4%)
    reduce_scatter x1, waiting for transfers between devices, shards(): lax.psum_scatter(term_gate.astype(jnp.bfloat16), 'dp', scatter_dimension=...  67.2 us
    reduce_scatter x1, waiting for transfers between devices, shards(): lax.psum_scatter(term_up.astype(jnp.bfloat16), 'dp', scatter_dimension=0,...  67.2 us
    all_gather x1, waiting for transfers between devices, shards(): lax.all_gather(w_gate, 'dp', axis=1, tiled=True)  43.8 us
    all_gather x1, waiting for transfers between devices, shards(): lax.all_gather(w_up, 'dp', axis=1, tiled=True)  43.8 us
    all_gather x1, waiting for transfers between devices, shards(): lax.all_gather(w_down, 'dp', axis=1, tiled=True)  29.3 us
    gather x6, local copies, waits for them, and re-layouts, shards(): back_in[rows_pick].astype(jnp.float32)  12.2 us
    gather x6, local copies, waits for them, and re-layouts, shards(): back_out[rows_pick].astype(jnp.float32)  10.4 us
    reduce_scatter x1, waiting for transfers between devices, shards(): lax.psum_scatter(term_down.astype(jnp.bfloat16), 'dp', scatter_dimension=...  8.88 us
  transfers between devices with their start and end apart: 10, of which 9 were waited for; matrix products, arithmetic and copies ran while one was open for 16% of the time, Pallas kernels for 0%

commit v1 on v0

v1 whole, which is shorter than its diff:
```python
import jax
import jax.numpy as jnp
from jax import lax
from jax.experimental import pallas as pl
from jax.experimental.pallas import tpu as pltpu
from jax.sharding import PartitionSpec as P

CAP = 32
CORES = 2
HALVES = 2
VMEM_BYTES = 48 * 1024 * 1024

CONTRACT_LAST = (((1,), (1,)), ((), ()))
CONTRACT_FIRST = (((0,), (0,)), ((), ()))


def call(kernel, out_shape, args, scratch=(), flops=0):
    moved = sum(a.size * a.dtype.itemsize for a in args) + sum(
        o.size * o.dtype.itemsize for o in out_shape
    )
    return pl.pallas_call(
        kernel,
        out_shape=out_shape,
        in_specs=[pl.BlockSpec(memory_space=pltpu.SMEM)]
        + [pl.BlockSpec(memory_space=pltpu.VMEM)] * (len(args) - 1),
        out_specs=[pl.BlockSpec(memory_space=pltpu.VMEM)] * len(out_shape),
        scratch_shapes=list(scratch),
        compiler_params=pltpu.CompilerParams(vmem_limit_bytes=VMEM_BYTES),
        cost_estimate=pl.CostEstimate(flops=flops, bytes_accessed=moved, transcendentals=0),
    )(*args)


def matches(routes, expert):
    return jnp.sum(jnp.where(routes == expert, 1.0, 0.0), axis=1, keepdims=True)


def chosen(routes, scale, expert):
    count = routes.shape[0]
    hit = matches(routes, expert)
    row = lax.broadcasted_iota(jnp.int32, (count, count), 0)
    column = lax.broadcasted_iota(jnp.int32, (count, count), 1)
    earlier = jnp.where(column < row, 1.0, 0.0).astype(jnp.bfloat16)
    place = jnp.dot(
        earlier,
        jnp.broadcast_to(hit, (count, 128)).astype(jnp.bfloat16),
        preferred_element_type=jnp.float32,
    )
    place = jnp.where(hit > 0.0, place[:, :1], -1.0).astype(jnp.int32)
    total = jnp.sum(scale, axis=1, keepdims=True)
    weight = jnp.sum(jnp.where(routes == expert, scale / total, 0.0), axis=1, keepdims=True)
    return place, weight


def selector(place):
    slots = lax.broadcasted_iota(jnp.int32, (place.shape[0], CAP), 1)
    return jnp.where(slots == place, 1.0, 0.0)


def shards(tokens, routes, gate_scale, w_gate, w_up, w_down, d_out):
    experts = lax.axis_size("expert")
    members = lax.axis_size("dp")
    chips = members // (HALVES * CORES)
    count, width = tokens.shape
    span = width // HALVES
    block, inner = w_gate.shape[1:]
    rows = experts * CAP
    bf16, f32 = jnp.bfloat16, jnp.float32
    spots = [(h, s) for h in range(HALVES) for s in range(experts)]

    member = lax.axis_index("dp")
    here = jnp.stack(
        [
            member // (chips * CORES),
            member // CORES % chips,
            member % CORES,
            lax.axis_index("expert"),
        ]
    ).astype(jnp.int32)

    def send(value, half=0, chip=0, core=0, shift=0):
        perm = []
        for d in range(members):
            to = d ^ (half * chips * CORES + chip * CORES + core)
            for e in range(experts):
                perm.append((d * experts + e, to * experts + (e + shift) % experts))
        return lax.ppermute(value, ("dp", "expert"), perm)

    def shape(*dims, dtype=bf16):
        return jax.ShapeDtypeStruct(dims, dtype)

    packed = jnp.concatenate([w_gate, w_up, w_down], axis=0)
    mine = [packed] + [send(packed, chip=o) for o in range(1, chips)]

    def dispatch(at, r_ref, s_ref, t_ref, d_ref, *outs):
        route, scale = r_ref[...], s_ref[...]
        for s in range(experts):
            expert = lax.rem(at[3] + s, experts)
            place, weight = chosen(route, scale, expert)
            pick = selector(place).astype(bf16)
            for h in range(HALVES):
                side = jnp.bitwise_xor(at[0], h)
                cols = pl.ds(pl.multiple_of(side * span, span), span)
                scaled = (d_ref[:, cols].astype(f32) * weight).astype(bf16)
                out = outs[h * experts + s]
                out[0] = lax.dot_general(
                    pick, t_ref[:, cols], CONTRACT_FIRST, preferred_element_type=f32
                ).astype(bf16)
                out[1] = lax.dot_general(
                    pick, scaled, CONTRACT_FIRST, preferred_element_type=f32
                ).astype(bf16)
            outs[-2][:, s : s + 1] = place
            outs[-1][:, s : s + 1] = weight

    *cut, places, weights = call(
        dispatch,
        [shape(2, CAP, span)] * len(spots)
        + [shape(count, experts, dtype=jnp.int32), shape(count, experts, dtype=f32)],
        [here, routes, gate_scale, tokens, d_out],
    )
    pieces = [cut[0]] + [
        send(cut[i], half=h, shift=s) for i, (h, s) in enumerate(spots) if i > 0
    ]
    theirs = [send(m, core=1) for m in mine]

    def gather_weights(at, refs, held):
        for i, ref in enumerate(refs):
            chip, core = i % chips, i // chips
            start = (jnp.bitwise_xor(at[1], chip) * CORES + jnp.bitwise_xor(at[2], core)) * block
            for m in range(3):
                held[m, pl.ds(pl.multiple_of(start, block), block), :] = ref[m]

    def project(at, *refs):
        ins, refs = refs[: len(spots)], refs[len(spots) :]
        ws, refs = refs[: chips * CORES], refs[chips * CORES :]
        keep, give, stay, leave, held = refs
        gather_weights(at, ws, held)
        x = jnp.concatenate([ref[0] for ref in ins], axis=0)
        d = jnp.concatenate([ref[1] for ref in ins], axis=0)
        for m, left in enumerate((x, x, d)):
            part = jnp.dot(left, held[m], preferred_element_type=f32)
            keep[m] = part[:rows]
            give[m] = part[rows:].astype(bf16)
        first = at[2] == 0
        for k in range(2):
            for i, ref in enumerate(ins):
                for chip in range(chips):
                    both = ref[k, :, chip * CORES * block : (chip + 1) * CORES * block]
                    low, high = both[:, :block], both[:, block:]
                    place = (k, slice(i * CAP, (i + 1) * CAP), slice(chip * block, (chip + 1) * block))
                    stay[place] = jnp.where(first, low, high)
                    leave[place] = jnp.where(first, high, low)

    keep, give, stay, leave = call(
        project,
        [
            shape(3, rows, inner, dtype=f32),
            shape(3, rows, inner),
            shape(2, HALVES * rows, chips * block),
            shape(2, HALVES * rows, chips * block),
        ],
        [here, *pieces, *mine, *theirs],
        scratch=[pltpu.VMEM((3, span, inner), bf16)],
        flops=2 * 3 * HALVES * rows * span * inner,
    )
    came = send(give, half=1)
    across = send(leave, core=1)

    def activate(at, keep_ref, came_ref, out):
        gate = keep_ref[0] + came_ref[0].astype(f32)
        up = keep_ref[1] + came_ref[1].astype(f32)
        d_hidden = keep_ref[2] + came_ref[2].astype(f32)
        sig = jax.nn.sigmoid(gate)
        act = gate * sig
        out[0] = (d_hidden * up * sig * (1.0 + gate * (1.0 - sig))).astype(bf16)
        out[1] = (d_hidden * act).astype(bf16)
        out[2] = (act * up).astype(bf16)

    (inside,) = call(activate, [shape(3, rows, inner)], [here, keep, came])
    other = send(inside, half=1)
    inside_c = send(inside, core=1)
    other_c = send(other, core=1)

    def weigh(at, a0, a1, a2, a3, x0, x1, *refs):
        outs, held = refs[:-1], refs[-1]
        for m in range(3):
            left = jnp.concatenate([x0[m // 2], x1[m // 2]], axis=0)
            right = jnp.concatenate([a0[m], a1[m], a2[m], a3[m]], axis=0)
            held[...] = lax.dot_general(left, right, CONTRACT_FIRST, preferred_element_type=f32)
            for o, out in enumerate(outs):
                start = pl.multiple_of(jnp.bitwise_xor(at[1], o) * block, block)
                out[m] = held[pl.ds(start, block), :].astype(out.dtype)

    grads = call(
        weigh,
        [shape(3, block, inner, dtype=f32)] + [shape(3, block, inner)] * (chips - 1),
        [here, inside, other, inside_c, other_c, stay, across],
        scratch=[pltpu.VMEM((chips * block, inner), f32)],
        flops=2 * 3 * CORES * HALVES * rows * chips * block * inner,
    )
    arrived = [send(grads[o], chip=o) for o in range(1, chips)]

    def expand(at, a0, a1, *refs):
        ws, outs, held = refs[: chips * CORES], refs[chips * CORES : -1], refs[-1]
        gather_weights(at, ws, held)
        part = [jnp.concatenate([a0[m], a1[m]], axis=0) for m in range(3)]
        out = lax.dot_general(part[2], held[2], CONTRACT_LAST, preferred_element_type=f32)
        d_in = lax.dot_general(
            part[0], held[0], CONTRACT_LAST, preferred_element_type=f32
        ) + lax.dot_general(part[1], held[1], CONTRACT_LAST, preferred_element_type=f32)
        for i, ref in enumerate(outs):
            ref[0] = out[i * CAP : (i + 1) * CAP].astype(bf16)
            ref[1] = d_in[i * CAP : (i + 1) * CAP].astype(bf16)

    back = call(
        expand,
        [shape(2, CAP, span)] * len(spots),
        [here, inside, other, *mine, *theirs],
        scratch=[pltpu.VMEM((3, span, inner), bf16)],
        flops=2 * 3 * HALVES * rows * span * inner,
    )
    home = [back[0]] + [
        send(back[i], half=h, shift=-s) for i, (h, s) in enumerate(spots) if i > 0
    ]

    def collect(at, p_ref, w_ref, *refs):
        ins, (out, d_in) = refs[: len(spots)], refs[len(spots) :]
        picks = [selector(p_ref[:, s : s + 1]).astype(bf16) for s in range(experts)]
        for h in range(HALVES):
            side = jnp.bitwise_xor(at[0], h)
            cols = pl.ds(pl.multiple_of(side * span, span), span)
            total_out = jnp.zeros((count, span), f32)
            total_in = jnp.zeros((count, span), f32)
            for s in range(experts):
                ref = ins[h * experts + s]
                total_out += w_ref[:, s : s + 1] * jnp.dot(
                    picks[s], ref[0], preferred_element_type=f32
                )
                total_in += jnp.dot(picks[s], ref[1], preferred_element_type=f32)
            out[:, cols] = total_out.astype(bf16)
            d_in[:, cols] = total_in.astype(bf16)

    layer_out, d_tokens = call(
        collect, [shape(count, width)] * 2, [here, places, weights, *home]
    )

    def finish(at, own, *refs):
        ins, outs = refs[: chips - 1], refs[chips - 1 :]
        for m, out in enumerate(outs):
            total = own[m]
            for ref in ins:
                total = total + ref[m].astype(f32)
            out[0] = total

    grad_gate, grad_up, grad_down = call(
        finish, [shape(1, block, inner, dtype=f32)] * 3, [here, grads[0], *arrived]
    )
    return layer_out, d_tokens, grad_gate, grad_up, grad_down


def solution(mesh):
    by_token = P(("dp", "expert"), None)
    by_expert = P("expert", "dp", None)
    return jax.shard_map(
        shards,
        mesh=mesh,
        in_specs=(by_token,) * 3 + (by_expert,) * 3 + (by_token,),
        out_specs=(by_token,) * 2 + (by_expert,) * 3,
        check_vma=False,
    )
```

time: 369 us -> 141 us (0.38)
  the two profiles are of different devices: /device:TPU:0 before, /device:TPU:8 now
where the time goes in v1:
time: 141 us; the launch traced here: 140 us
  waiting for transfers between devices  79.5 us (56%)
  starting transfers between devices  36.6 us (26%)
  Pallas kernels  14 us (10%)
  local copies, waits for them, and re-layouts  9.23 us (7%)
    ppermute x21, waiting for transfers between devices, send(): return lax.ppermute(value, ('dp', 'expert'), perm)  79.5 us
    ppermute x21, starting transfers between devices, send(): return lax.ppermute(value, ('dp', 'expert'), perm)  36.6 us
    pallas_call x7, Pallas kernels, call(): pl.pallas_call(kernel, out_shape=out_shape, in_specs=[pl.BlockSpec(memory...  14 us
    unnamed x20, local copies, waits for them, and re-layouts  8.29 us
  transfers between devices with their start and end apart: 21, of which 11 were waited for; matrix products, arithmetic and copies ran while one was open for 1% of the time, Pallas kernels for 5%

profile of v1, /device:TPU:8, one launch (start us, length us, event | category | flops | bytes accessed | tf_op | source)
XLA Modules:
  0.0 140.3 jit_solution(8413453596883869128)
XLA Ops:
  5.0 1.6 %collective-permute-start.4 = (bf16[3,128,768]{2,1,0:T(8,128)(2,1)S(1)}, bf16[3,128,768]{2,1,0:T(8,128)(2,1)S(1)}, u32[]{:S(2)}, u32[]{:S(2)}) collective-permute-start(bf16[3,128,768]{2,1,0:T(8,128)(2,1)S(1)} %constant_dynamic-update-slice_fusion.refs_4_.refs_0_), channel_id=1, source_target_pairs={{0,8},{1,9},{2,10},{3,11},{4,12},{5,13},{6,14},{7,15},{8,0},{9,1},... | collective-permute-start | bytes 1769480 | tf_op jit(solution)/shard_map/ppermute | solution.py:86
  7.1 13.7 %collective-permute-done.5.refs_7_.refs_3_ = bf16[3,128,768]{2,1,0:T(8,128)(2,1)S(1)} collective-permute-done((bf16[3,128,768]{2,1,0:T(8,128)(2,1)S(1)}, bf16[3,128,768]{2,1,0:T(8,128)(2,1)S(1)}, u32[]{:S(2)}, u32[]{:S(2)}) %collective-permute-start.5) | collective-permute-done | bytes 589856 | tf_op jit(solution)/shard_map/ppermute | solution.py:86
  20.7 11.5 %collective-permute-done.4.refs_6_.refs_2_ = bf16[3,128,768]{2,1,0:T(8,128)(2,1)S(1)} collective-permute-done((bf16[3,128,768]{2,1,0:T(8,128)(2,1)S(1)}, bf16[3,128,768]{2,1,0:T(8,128)(2,1)S(1)}, u32[]{:S(2)}, u32[]{:S(2)}) %collective-permute-start.4) | collective-permute-done | bytes 589856 | tf_op jit(solution)/shard_map/ppermute | solution.py:86
  38.5 1.8 %shard_map.110 = (bf16[2,32,1024]{2,1,0:T(8,128)(2,1)S(1)}, bf16[2,32,1024]{2,1,0:T(8,128)(2,1)S(1)}, bf16[2,32,1024]{2,1,0:T(8,128)(2,1)S(1)}, bf16[2,32,1024]{...) custom-call(s32[4]{0:T(128)S(1)} %pad_add_fusion.at, s32[192,6]{1,0:T(8,128)S(1)} %copy-done.4, ...), custom_call_target="tpu_custom_call" | custom-call | bytes 2109456 | tf_op jit(solution)/shard_map/pallas_call | solution.py:21
  41.8 3.9 %collective-permute-done.refs_1_ = bf16[2,32,1024]{2,1,0:T(8,128)(2,1)S(1)} collective-permute-done((bf16[2,32,1024]{2,1,0:T(8,128)(2,1)S(1)}, bf16[2,32,1024]{2,1,0:T(8,128)(2,1)S(1)}, u32[]{:S(2)}, u32[]{:S(2)}) %collective-permute-start) | collective-permute-done | bytes 131104 | tf_op jit(solution)/shard_map/ppermute | solution.py:86
  45.7 2.6 %collective-permute-start.1 = (bf16[2,32,1024]{2,1,0:T(8,128)(2,1)S(1)}, bf16[2,32,1024]{2,1,0:T(8,128)(2,1)S(1)}, u32[]{:S(2)}, u32[]{:S(2)}) collective-permute-start(bf16[2,32,1024]{2,1,0:T(8,128)(2,1)S(1)} %get-tuple-element.32), channel_id=1, source_target_pairs={{0,16},{1,17},{2,18},{3,19},{4,20},{5,21},{6,22},{7,23},{8,24},{9,... | collective-permute-start | bytes 393224 | tf_op jit(solution)/shard_map/ppermute | solution.py:86
  48.3 4.8 %collective-permute-done.1.refs_2_ = bf16[2,32,1024]{2,1,0:T(8,128)(2,1)S(1)} collective-permute-done((bf16[2,32,1024]{2,1,0:T(8,128)(2,1)S(1)}, bf16[2,32,1024]{2,1,0:T(8,128)(2,1)S(1)}, u32[]{:S(2)}, u32[]{:S(2)}) %collective-permute-start.1) | collective-permute-done | bytes 131104 | tf_op jit(solution)/shard_map/ppermute | solution.py:86
  53.1 4.3 %collective-permute-start.2 = (bf16[2,32,1024]{2,1,0:T(8,128)(2,1)S(1)}, bf16[2,32,1024]{2,1,0:T(8,128)(2,1)S(1)}, u32[]{:S(2)}, u32[]{:S(2)}) collective-permute-start(bf16[2,32,1024]{2,1,0:T(8,128)(2,1)S(1)} %get-tuple-element.33), channel_id=1, source_target_pairs={{0,17},{1,16},{2,19},{3,18},{4,21},{5,20},{6,23},{7,22},{8,25},{9,... | collective-permute-start | bytes 393224 | tf_op jit(solution)/shard_map/ppermute | solution.py:86
  57.4 3.4 %collective-permute-done.2.refs_3_ = bf16[2,32,1024]{2,1,0:T(8,128)(2,1)S(1)} collective-permute-done((bf16[2,32,1024]{2,1,0:T(8,128)(2,1)S(1)}, bf16[2,32,1024]{2,1,0:T(8,128)(2,1)S(1)}, u32[]{:S(2)}, u32[]{:S(2)}) %collective-permute-start.2) | collective-permute-done | bytes 131104 | tf_op jit(solution)/shard_map/ppermute | solution.py:86
  61.6 2.5 %shard_map.111 = (f32[3,64,768]{2,1,0:T(8,128)S(1)}, bf16[3,64,768]{2,1,0:T(8,128)(2,1)S(1)}, bf16[2,128,512]{2,1,0:T(8,128)(2,1)S(1)}, bf16[2,128,512]{2,1,0:T(8,128)(2,1)S(1)}) custom-call(s32[4]{0:T(128)S(1)} %pad_add_fusion.at, bf16[2,32,1024]{2,1,0:T(8,128)(2,1)S(1)} %get-tuple-element.30.refs_0_, ...), custom_call_target="tpu_custom_call" | custom-call | flops 603979776 | bytes 6651920 | tf_op jit(solution)/shard_map/pallas_call | solution.py:21
  64.1 2.9 %collective-permute-start.10 = (bf16[3,64,768]{2,1,0:T(8,128)(2,1)S(1)}, bf16[3,64,768]{2,1,0:T(8,128)(2,1)S(1)}, u32[]{:S(2)}, u32[]{:S(2)}) collective-permute-start(bf16[3,64,768]{2,1,0:T(8,128)(2,1)S(1)} %get-tuple-element.35), channel_id=1, source_target_pairs={{0,16},{1,17},{2,18},{3,19},{4,20},{5,21},{6,22},{7,23},{8,24},{9,... | collective-permute-start | bytes 884744 | tf_op jit(solution)/shard_map/ppermute | solution.py:86
  67.1 10.7 %collective-permute-done.10.came_ref = bf16[3,64,768]{2,1,0:T(8,128)(2,1)S(1)} collective-permute-done((bf16[3,64,768]{2,1,0:T(8,128)(2,1)S(1)}, bf16[3,64,768]{2,1,0:T(8,128)(2,1)S(1)}, u32[]{:S(2)}, u32[]{:S(2)}) %collective-permute-start.10) | collective-permute-done | bytes 294944 | tf_op jit(solution)/shard_map/ppermute | solution.py:86
  78.4 9.7 %collective-permute-start.11 = (bf16[3,64,768]{2,1,0:T(8,128)(2,1)S(1)}, bf16[3,64,768]{2,1,0:T(8,128)(2,1)S(1)}, u32[]{:S(2)}, u32[]{:S(2)}) collective-permute-start(bf16[3,64,768]{2,1,0:T(8,128)(2,1)S(1)} %shard_map.112.a0), channel_id=1, source_target_pairs={{0,16},{1,17},{2,18},{3,19},{4,20},{5,21},{6,22},{7,23},{8,24},{9,... | collective-permute-start | bytes 884744 | tf_op jit(solution)/shard_map/ppermute | solution.py:86
  88.2 7.2 %collective-permute-done.11.a1 = bf16[3,64,768]{2,1,0:T(8,128)(2,1)S(1)} collective-permute-done((bf16[3,64,768]{2,1,0:T(8,128)(2,1)S(1)}, bf16[3,64,768]{2,1,0:T(8,128)(2,1)S(1)}, u32[]{:S(2)}, u32[]{:S(2)}) %collective-permute-start.11) | collective-permute-done | bytes 294944 | tf_op jit(solution)/shard_map/ppermute | solution.py:86
  97.3 1.7 %shard_map.115 = (f32[3,128,768]{2,1,0:T(8,128)S(1)}, bf16[3,128,768]{2,1,0:T(8,128)(2,1)S(1)}, bf16[3,128,768]{2,1,0:T(8,128)(2,1)S(1)}, bf16[3,128,768]{2,1,0:T(8,128)(2,1)S(1)}) custom-call(s32[4]{0:T(128)S(1)} %pad_add_fusion.at, bf16[3,64,768]{2,1,0:T(8,128)(2,1)S(1)} %shard_map.112.a0, bf16[3,64,768]{2,1,0:T(8,128)(2,1)S(1)} %collective-permute-done.11.a1, ...), custom_call_target="tpu_custom_call" | custom-call | flops 603979776 | bytes 4653072 | tf_op jit(solution)/shard_map/pallas_call | solution.py:21
  99.1 3.4 %collective-permute-start.20 = (bf16[3,128,768]{2,1,0:T(8,128)(2,1)S(1)}, bf16[3,128,768]{2,1,0:T(8,128)(2,1)S(1)}, u32[]{:S(2)}, u32[]{:S(2)}) collective-permute-start(bf16[3,128,768]{2,1,0:T(8,128)(2,1)S(1)} %get-tuple-element.47), channel_id=1, source_target_pairs={{0,12},{1,13},{2,14},{3,15},{4,8},{5,9},{6,10},{7,11},{8,4},{9,5},... | collective-permute-start | bytes 1769480 | tf_op jit(solution)/shard_map/ppermute | solution.py:86
  102.5 3.2 %shard_map.113 = (bf16[2,32,1024]{2,1,0:T(8,128)(2,1)S(1)}, bf16[2,32,1024]{2,1,0:T(8,128)(2,1)S(1)}, bf16[2,32,1024]{2,1,0:T(8,128)(2,1)S(1)}, bf16[2,32,1024]{2,1,0:T(8,128)(2,1)S(1)}) custom-call(s32[4]{0:T(128)S(1)} %pad_add_fusion.at, bf16[3,64,768]{2,1,0:T(8,128)(2,1)S(1)} %shard_map.112.a0, bf16[3,64,768]{2,1,0:T(8,128)(2,1)S(1)} %collective-permute-done.11.a1, ...), custom_call_target="tpu_custom_call" | custom-call | flops 603979776 | bytes 5832720 | tf_op jit(solution)/shard_map/pallas_call | solution.py:21
  105.7 1.9 %collective-permute-start.12 = (bf16[2,32,1024]{2,1,0:T(8,128)(2,1)S(1)}, bf16[2,32,1024]{2,1,0:T(8,128)(2,1)S(1)}, u32[]{:S(2)}, u32[]{:S(2)}) collective-permute-start(bf16[2,32,1024]{2,1,0:T(8,128)(2,1)S(1)} %get-tuple-element.37), channel_id=1, source_target_pairs={{0,1},{1,0},{2,3},{3,2},{4,5},{5,4},{6,7},{7,6},{8,9},{9,8},{10,11... | collective-permute-start | bytes 393224 | tf_op jit(solution)/shard_map/ppermute | solution.py:86
  107.6 2.2 %collective-permute-start.13 = (bf16[2,32,1024]{2,1,0:T(8,128)(2,1)S(1)}, bf16[2,32,1024]{2,1,0:T(8,128)(2,1)S(1)}, u32[]{:S(2)}, u32[]{:S(2)}) collective-permute-start(bf16[2,32,1024]{2,1,0:T(8,128)(2,1)S(1)} %get-tuple-element.38), channel_id=1, source_target_pairs={{0,16},{1,17},{2,18},{3,19},{4,20},{5,21},{6,22},{7,23},{8,24},{9,... | collective-permute-start | bytes 393224 | tf_op jit(solution)/shard_map/ppermute | solution.py:86
  110.9 3.3 %collective-permute-start.14 = (bf16[2,32,1024]{2,1,0:T(8,128)(2,1)S(1)}, bf16[2,32,1024]{2,1,0:T(8,128)(2,1)S(1)}, u32[]{:S(2)}, u32[]{:S(2)}) collective-permute-start(bf16[2,32,1024]{2,1,0:T(8,128)(2,1)S(1)} %get-tuple-element.39), channel_id=1, source_target_pairs={{0,17},{1,16},{2,19},{3,18},{4,21},{5,20},{6,23},{7,22},{8,25},{9,... | collective-permute-start | bytes 393224 | tf_op jit(solution)/shard_map/ppermute | solution.py:86
  114.2 17.1 %collective-permute-done.13.refs_2_ = bf16[2,32,1024]{2,1,0:T(8,128)(2,1)S(1)} collective-permute-done((bf16[2,32,1024]{2,1,0:T(8,128)(2,1)S(1)}, bf16[2,32,1024]{2,1,0:T(8,128)(2,1)S(1)}, u32[]{:S(2)}, u32[]{:S(2)}) %collective-permute-start.13) | collective-permute-done | bytes 131104 | tf_op jit(solution)/shard_map/ppermute | solution.py:86
  131.3 4.7 %collective-permute-done.14.refs_3_ = bf16[2,32,1024]{2,1,0:T(8,128)(2,1)S(1)} collective-permute-done((bf16[2,32,1024]{2,1,0:T(8,128)(2,1)S(1)}, bf16[2,32,1024]{2,1,0:T(8,128)(2,1)S(1)}, u32[]{:S(2)}, u32[]{:S(2)}) %collective-permute-start.14) | collective-permute-done | bytes 131104 | tf_op jit(solution)/shard_map/ppermute | solution.py:86
  136.0 2.5 %shard_map.114 = (bf16[192,2048]{1,0:T(8,128)(2,1)}, bf16[192,2048]{1,0:T(8,128)(2,1)}) custom-call(s32[4]{0:T(128)S(1)} %pad_add_fusion.at, s32[192,2]{1,0:T(8,128)S(1)} %get-tuple-element.28.p_ref, f32[192,2]{1,0:T(8,128)S(1)} %get-tuple-element.29.w_ref, bf16[2,32,1024]{2,1,0:T(8,128)(2,1)S(1)} %get-tuple-element.36.refs_0_, ...), custom_call_target="tpu_custom_call" | custom-call | bytes 2100240 | tf_op jit(solution)/shard_map/pallas_call | solution.py:21
  138.6 1.7 %shard_map.116 = (f32[1,128,768]{2,1,0:T(8,128)}, f32[1,128,768]{2,1,0:T(8,128)}, f32[1,128,768]{2,1,0:T(8,128)}) custom-call(s32[4]{0:T(128)S(1)} %pad_add_fusion.at, f32[3,128,768]{2,1,0:T(8,128)S(1)} %get-tuple-element.44.own, bf16[3,128,768]{2,1,0:T(8,128)(2,1)S(1)} %collective-permute-done.18.refs_0_, ...), custom_call_target="tpu_custom_call" | custom-call | bytes 4128784 | tf_op jit(solution)/shard_map/pallas_call | solution.py:21
  (47 shorter events, 17.2 us)
Async XLA Ops:
  0.6 32.2 %copy-start.6 = (s32[192,6]{0,1:T(8,128)S(1)}, s32[192,6]{0,1:T(8,128)}, u32[]{:S(2)}) copy-start(s32[192,6]{0,1:T(8,128)} %param.8) | copy-start | bytes 13828
  0.6 32.9 %copy-start.7 = (f32[192,6]{0,1:T(8,128)S(1)}, f32[192,6]{0,1:T(8,128)}, u32[]{:S(2)}) copy-start(f32[192,6]{0,1:T(8,128)} %param.9) | copy-start | bytes 13828
  3.5 17.2 %collective-permute-start.5 = (bf16[3,128,768]{2,1,0:T(8,128)(2,1)S(1)}, bf16[3,128,768]{2,1,0:T(8,128)(2,1)S(1)}, u32[]{:S(2)}, u32[]{:S(2)}) collective-permute-start(bf16[3,128,768]{2,1,0:T(8,128)(2,1)S(1)} %constant_dynamic-update-slice_fusion.refs_4_.refs_0_), channel_id=1, source_target_pairs={{0,12},{1,13},{2,14},{3,15},{4,8},{5,9},{6,10},{7,11},{8,4},{9,5},... | collective-permute-start | bytes 1769480 | tf_op jit(solution)/shard_map/ppermute | solution.py:86
  5.0 27.3 %collective-permute-start.4 = (bf16[3,128,768]{2,1,0:T(8,128)(2,1)S(1)}, bf16[3,128,768]{2,1,0:T(8,128)(2,1)S(1)}, u32[]{:S(2)}, u32[]{:S(2)}) collective-permute-start(bf16[3,128,768]{2,1,0:T(8,128)(2,1)S(1)} %constant_dynamic-update-slice_fusion.refs_4_.refs_0_), channel_id=1, source_target_pairs={{0,8},{1,9},{2,10},{3,11},{4,12},{5,13},{6,14},{7,15},{8,0},{9,1},... | collective-permute-start | bytes 1769480 | tf_op jit(solution)/shard_map/ppermute | solution.py:86
  6.5 25.7 %collective-permute-start.3 = (bf16[3,128,768]{2,1,0:T(8,128)(2,1)S(1)}, bf16[3,128,768]{2,1,0:T(8,128)(2,1)S(1)}, u32[]{:S(2)}, u32[]{:S(2)}) collective-permute-start(bf16[3,128,768]{2,1,0:T(8,128)(2,1)S(1)} %constant_dynamic-update-slice_fusion.refs_4_.refs_0_), channel_id=1, source_target_pairs={{0,4},{1,5},{2,6},{3,7},{4,0},{5,1},{6,2},{7,3},{8,12},{9,13},{10,... | collective-permute-start | bytes 1769480 | tf_op jit(solution)/shard_map/ppermute | solution.py:86
  7.1 53.7 %collective-permute-start.6 = (bf16[3,128,768]{2,1,0:T(8,128)(2,1)S(1)}, bf16[3,128,768]{2,1,0:T(8,128)(2,1)S(1)}, u32[]{:S(2)}, u32[]{:S(2)}) collective-permute-start(bf16[3,128,768]{2,1,0:T(8,128)(2,1)S(1)} %constant_dynamic-update-slice_fusion.refs_4_.refs_0_), channel_id=1, source_target_pairs={{0,2},{1,3},{2,0},{3,1},{4,6},{5,7},{6,4},{7,5},{8,10},{9,11},{10,... | collective-permute-start | bytes 1769480 | tf_op jit(solution)/shard_map/ppermute | solution.py:86
  20.7 40.1 %collective-permute-start.9 = (bf16[3,128,768]{2,1,0:T(8,128)(2,1)S(1)}, bf16[3,128,768]{2,1,0:T(8,128)(2,1)S(1)}, u32[]{:S(2)}, u32[]{:S(2)}) collective-permute-start(bf16[3,128,768]{2,1,0:T(8,128)(2,1)S(1)} %collective-permute-done.5.refs_7_.refs_3_), channel_id=1, source_target_pairs={{0,2},{1,3},{2,0},{3,1},{4,6},{5,7},{6,4},{7,5},{8,10},{9,11},{10,... | collective-permute-start | bytes 1769480 | tf_op jit(solution)/shard_map/ppermute | solution.py:86
  32.3 28.5 %collective-permute-start.8 = (bf16[3,128,768]{2,1,0:T(8,128)(2,1)S(1)}, bf16[3,128,768]{2,1,0:T(8,128)(2,1)}, u32[]{:S(2)}, u32[]{:S(2)}) collective-permute-start(bf16[3,128,768]{2,1,0:T(8,128)(2,1)S(1)} %collective-permute-done.4.refs_6_.refs_2_), channel_id=1, source_target_pairs={{0,2},{1,3},{2,0},{3,1},{4,6},{5,7},{6,4},{7,5},{8,10},{9,11},{10,... | collective-permute-start | bytes 1769480 | tf_op jit(solution)/shard_map/ppermute | solution.py:86
  32.3 28.5 %collective-permute-start.7 = (bf16[3,128,768]{2,1,0:T(8,128)(2,1)S(1)}, bf16[3,128,768]{2,1,0:T(8,128)(2,1)}, u32[]{:S(2)}, u32[]{:S(2)}) collective-permute-start(bf16[3,128,768]{2,1,0:T(8,128)(2,1)S(1)} %collective-permute-done.3.refs_5_.refs_1_), channel_id=1, source_target_pairs={{0,2},{1,3},{2,0},{3,1},{4,6},{5,7},{6,4},{7,5},{8,10},{9,11},{10,... | collective-permute-start | bytes 1769480 | tf_op jit(solution)/shard_map/ppermute | solution.py:86
  40.2 5.5 %collective-permute-start = (bf16[2,32,1024]{2,1,0:T(8,128)(2,1)S(1)}, bf16[2,32,1024]{2,1,0:T(8,128)(2,1)S(1)}, u32[]{:S(2)}, u32[]{:S(2)}) collective-permute-start(bf16[2,32,1024]{2,1,0:T(8,128)(2,1)S(1)} %get-tuple-element.31), channel_id=1, source_target_pairs={{0,1},{1,0},{2,3},{3,2},{4,5},{5,4},{6,7},{7,6},{8,9},{9,8},{10,11... | collective-permute-start | bytes 393224 | tf_op jit(solution)/shard_map/ppermute | solution.py:86
  45.7 7.4 %collective-permute-start.1 = (bf16[2,32,1024]{2,1,0:T(8,128)(2,1)S(1)}, bf16[2,32,1024]{2,1,0:T(8,128)(2,1)S(1)}, u32[]{:S(2)}, u32[]{:S(2)}) collective-permute-start(bf16[2,32,1024]{2,1,0:T(8,128)(2,1)S(1)} %get-tuple-element.32), channel_id=1, source_target_pairs={{0,16},{1,17},{2,18},{3,19},{4,20},{5,21},{6,22},{7,23},{8,24},{9,... | collective-permute-start | bytes 393224 | tf_op jit(solution)/shard_map/ppermute | solution.py:86
  53.1 7.7 %collective-permute-start.2 = (bf16[2,32,1024]{2,1,0:T(8,128)(2,1)S(1)}, bf16[2,32,1024]{2,1,0:T(8,128)(2,1)S(1)}, u32[]{:S(2)}, u32[]{:S(2)}) collective-permute-start(bf16[2,32,1024]{2,1,0:T(8,128)(2,1)S(1)} %get-tuple-element.33), channel_id=1, source_target_pairs={{0,17},{1,16},{2,19},{3,18},{4,21},{5,20},{6,23},{7,22},{8,25},{9,... | collective-permute-start | bytes 393224 | tf_op jit(solution)/shard_map/ppermute | solution.py:86
  64.1 13.6 %collective-permute-start.10 = (bf16[3,64,768]{2,1,0:T(8,128)(2,1)S(1)}, bf16[3,64,768]{2,1,0:T(8,128)(2,1)S(1)}, u32[]{:S(2)}, u32[]{:S(2)}) collective-permute-start(bf16[3,64,768]{2,1,0:T(8,128)(2,1)S(1)} %get-tuple-element.35), channel_id=1, source_target_pairs={{0,16},{1,17},{2,18},{3,19},{4,20},{5,21},{6,22},{7,23},{8,24},{9,... | collective-permute-start | bytes 884744 | tf_op jit(solution)/shard_map/ppermute | solution.py:86
  78.4 24.1 %copy-start.1 = (bf16[3,128,768]{2,1,0:T(8,128)(2,1)S(1)}, bf16[3,128,768]{2,1,0:T(8,128)(2,1)}, u32[]{:S(2)}) copy-start(bf16[3,128,768]{2,1,0:T(8,128)(2,1)} %copy-done) | copy-start | bytes 1769476
  78.4 16.9 %collective-permute-start.11 = (bf16[3,64,768]{2,1,0:T(8,128)(2,1)S(1)}, bf16[3,64,768]{2,1,0:T(8,128)(2,1)S(1)}, u32[]{:S(2)}, u32[]{:S(2)}) collective-permute-start(bf16[3,64,768]{2,1,0:T(8,128)(2,1)S(1)} %shard_map.112.a0), channel_id=1, source_target_pairs={{0,16},{1,17},{2,18},{3,19},{4,20},{5,21},{6,22},{7,23},{8,24},{9,... | collective-permute-start | bytes 884744 | tf_op jit(solution)/shard_map/ppermute | solution.py:86
  88.2 9.2 %collective-permute-start.15 = (bf16[3,64,768]{2,1,0:T(8,128)(2,1)S(1)}, bf16[3,64,768]{2,1,0:T(8,128)(2,1)S(1)}, u32[]{:S(2)}, u32[]{:S(2)}) collective-permute-start(bf16[3,64,768]{2,1,0:T(8,128)(2,1)S(1)} %shard_map.112.a0), channel_id=1, source_target_pairs={{0,2},{1,3},{2,0},{3,1},{4,6},{5,7},{6,4},{7,5},{8,10},{9,11},{10,... | collective-permute-start | bytes 884744 | tf_op jit(solution)/shard_map/ppermute | solution.py:86
  95.4 2.0 %collective-permute-start.16 = (bf16[3,64,768]{2,1,0:T(8,128)(2,1)S(1)}, bf16[3,64,768]{2,1,0:T(8,128)(2,1)S(1)}, u32[]{:S(2)}, u32[]{:S(2)}) collective-permute-start(bf16[3,64,768]{2,1,0:T(8,128)(2,1)S(1)} %collective-permute-done.11.a1), channel_id=1, source_target_pairs={{0,2},{1,3},{2,0},{3,1},{4,6},{5,7},{6,4},{7,5},{8,10},{9,11},{10,... | collective-permute-start | bytes 884744 | tf_op jit(solution)/shard_map/ppermute | solution.py:86
  95.4 2.0 %collective-permute-start.17 = (bf16[2,128,512]{2,1,0:T(8,128)(2,1)S(1)}, bf16[2,128,512]{2,1,0:T(8,128)(2,1)S(1)}, u32[]{:S(2)}, u32[]{:S(2)}) collective-permute-start(bf16[2,128,512]{2,1,0:T(8,128)(2,1)S(1)} %get-tuple-element.43), channel_id=1, source_target_pairs={{0,2},{1,3},{2,0},{3,1},{4,6},{5,7},{6,4},{7,5},{8,10},{9,11},{10,... | collective-permute-start | bytes 786440 | tf_op jit(solution)/shard_map/ppermute | solution.py:86
  99.0 39.6 %collective-permute-start.18 = (bf16[3,128,768]{2,1,0:T(8,128)(2,1)S(1)}, bf16[3,128,768]{2,1,0:T(8,128)(2,1)S(1)}, u32[]{:S(2)}, u32[]{:S(2)}) collective-permute-start(bf16[3,128,768]{2,1,0:T(8,128)(2,1)S(1)} %get-tuple-element.45), channel_id=1, source_target_pairs={{0,4},{1,5},{2,6},{3,7},{4,0},{5,1},{6,2},{7,3},{8,12},{9,13},{10,... | collective-permute-start | bytes 1769480 | tf_op jit(solution)/shard_map/ppermute | solution.py:86
  99.1 39.5 %collective-permute-start.19 = (bf16[3,128,768]{2,1,0:T(8,128)(2,1)S(1)}, bf16[3,128,768]{2,1,0:T(8,128)(2,1)S(1)}, u32[]{:S(2)}, u32[]{:S(2)}) collective-permute-start(bf16[3,128,768]{2,1,0:T(8,128)(2,1)S(1)} %get-tuple-element.46), channel_id=1, source_target_pairs={{0,8},{1,9},{2,10},{3,11},{4,12},{5,13},{6,14},{7,15},{8,0},{9,1},... | collective-permute-start | bytes 1769480 | tf_op jit(solution)/shard_map/ppermute | solution.py:86
  99.1 39.4 %collective-permute-start.20 = (bf16[3,128,768]{2,1,0:T(8,128)(2,1)S(1)}, bf16[3,128,768]{2,1,0:T(8,128)(2,1)S(1)}, u32[]{:S(2)}, u32[]{:S(2)}) collective-permute-start(bf16[3,128,768]{2,1,0:T(8,128)(2,1)S(1)} %get-tuple-element.47), channel_id=1, source_target_pairs={{0,12},{1,13},{2,14},{3,15},{4,8},{5,9},{6,10},{7,11},{8,4},{9,5},... | collective-permute-start | bytes 1769480 | tf_op jit(solution)/shard_map/ppermute | solution.py:86
  105.7 5.1 %collective-permute-start.12 = (bf16[2,32,1024]{2,1,0:T(8,128)(2,1)S(1)}, bf16[2,32,1024]{2,1,0:T(8,128)(2,1)S(1)}, u32[]{:S(2)}, u32[]{:S(2)}) collective-permute-start(bf16[2,32,1024]{2,1,0:T(8,128)(2,1)S(1)} %get-tuple-element.37), channel_id=1, source_target_pairs={{0,1},{1,0},{2,3},{3,2},{4,5},{5,4},{6,7},{7,6},{8,9},{9,8},{10,11... | collective-permute-start | bytes 393224 | tf_op jit(solution)/shard_map/ppermute | solution.py:86
  107.6 23.7 %collective-permute-start.13 = (bf16[2,32,1024]{2,1,0:T(8,128)(2,1)S(1)}, bf16[2,32,1024]{2,1,0:T(8,128)(2,1)S(1)}, u32[]{:S(2)}, u32[]{:S(2)}) collective-permute-start(bf16[2,32,1024]{2,1,0:T(8,128)(2,1)S(1)} %get-tuple-element.38), channel_id=1, source_target_pairs={{0,16},{1,17},{2,18},{3,19},{4,20},{5,21},{6,22},{7,23},{8,24},{9,... | collective-permute-start | bytes 393224 | tf_op jit(solution)/shard_map/ppermute | solution.py:86
  110.9 25.2 %collective-permute-start.14 = (bf16[2,32,1024]{2,1,0:T(8,128)(2,1)S(1)}, bf16[2,32,1024]{2,1,0:T(8,128)(2,1)S(1)}, u32[]{:S(2)}, u32[]{:S(2)}) collective-permute-start(bf16[2,32,1024]{2,1,0:T(8,128)(2,1)S(1)} %get-tuple-element.39), channel_id=1, source_target_pairs={{0,17},{1,16},{2,19},{3,18},{4,21},{5,20},{6,23},{7,22},{8,25},{9,... | collective-permute-start | bytes 393224 | tf_op jit(solution)/shard_map/ppermute | solution.py:86
  (5 other events, 4.9 us)

commit v2 on v1

v2 whole, which is shorter than its diff:
```python
import functools

import jax
import jax.numpy as jnp
from jax import lax
from jax.experimental import pallas as pl
from jax.experimental.pallas import tpu as pltpu
from jax.sharding import PartitionSpec as P

CAP = 32
CORES = 2
HALVES = 2
VMEM_BYTES = 48 * 1024 * 1024

CONTRACT_LAST = (((1,), (1,)), ((), ()))
CONTRACT_FIRST = (((0,), (0,)), ((), ()))


def call(kernel, out_shape, args, scratch=(), flops=0):
    moved = sum(a.size * a.dtype.itemsize for a in args) + sum(
        o.size * o.dtype.itemsize for o in out_shape
    )
    return pl.pallas_call(
        kernel,
        out_shape=out_shape,
        in_specs=[pl.BlockSpec(memory_space=pltpu.SMEM)]
        + [pl.BlockSpec(memory_space=pltpu.VMEM)] * (len(args) - 1),
        out_specs=[pl.BlockSpec(memory_space=pltpu.VMEM)] * len(out_shape),
        scratch_shapes=list(scratch),
        compiler_params=pltpu.CompilerParams(vmem_limit_bytes=VMEM_BYTES),
        cost_estimate=pl.CostEstimate(flops=flops, bytes_accessed=moved, transcendentals=0),
    )(*args)


def rank(hits):
    count = hits.shape[1]
    row = lax.broadcasted_iota(jnp.int32, (count, count), 0)
    column = lax.broadcasted_iota(jnp.int32, (count, count), 1)
    earlier = jnp.where(row < column, 1.0, 0.0).astype(jnp.bfloat16)
    return jnp.dot(hits.astype(jnp.bfloat16), earlier, preferred_element_type=jnp.float32)


def selector(place):
    slots = lax.broadcasted_iota(jnp.int32, (CAP, place.shape[1]), 0).astype(jnp.float32)
    return jnp.where(slots == place, 1.0, 0.0)


def shards(tokens, routes, gate_scale, w_gate, w_up, w_down, d_out):
    experts = lax.axis_size("expert")
    members = lax.axis_size("dp")
    chips = members // (HALVES * CORES)
    count, width = tokens.shape
    span = width // HALVES
    block, inner = w_gate.shape[1:]
    rows = experts * CAP
    bf16, f32 = jnp.bfloat16, jnp.float32
    spots = [(h, s) for h in range(HALVES) for s in range(experts)]

    member = lax.axis_index("dp")
    here = jnp.stack(
        [
            member // (chips * CORES),
            member // CORES % chips,
            member % CORES,
            lax.axis_index("expert"),
        ]
    ).astype(jnp.int32)

    def send(value, half=0, chip=0, core=0, shift=0):
        perm = []
        for d in range(members):
            to = d ^ (half * chips * CORES + chip * CORES + core)
            for e in range(experts):
                perm.append((d * experts + e, to * experts + (e + shift) % experts))
        return lax.ppermute(value, ("dp", "expert"), perm)

    def shape(*dims, dtype=bf16):
        return jax.ShapeDtypeStruct(dims, dtype)

    half_block = block // 2

    def pack(g_ref, u_ref, w_ref, out):
        for m, ref in enumerate((g_ref, u_ref, w_ref)):
            for k in range(2):
                out[k, m] = ref[0, k * half_block : (k + 1) * half_block]

    own = pl.pallas_call(pack, out_shape=shape(2, 3, half_block, inner))(w_gate, w_up, w_down)
    two_hops = chips == 4
    near = [send(own, chip=o) for o in range(1, chips - 1 if two_hops else chips)]
    own_c = send(own, core=1)

    def dispatch(at, r_ref, s_ref, t_ref, d_ref, *outs):
        *outs, p_ref, c_ref = outs
        route, scale = r_ref[...], s_ref[...]
        combine = scale / jnp.sum(scale, axis=0, keepdims=True)
        hits, weights = [], []
        for s in range(experts):
            match = route == lax.rem(at[3] + s, experts)
            hits.append(jnp.sum(jnp.where(match, 1.0, 0.0), axis=0, keepdims=True))
            weights.append(jnp.sum(jnp.where(match, combine, 0.0), axis=0, keepdims=True))
        pad = [jnp.zeros((8 - experts, count), f32)] if experts < 8 else []
        hits = jnp.concatenate(hits + pad, axis=0)
        places = jnp.where(hits > 0.0, rank(hits), -1.0)
        p_ref[...] = places
        c_ref[...] = jnp.concatenate(weights + pad, axis=0)
        for s in range(experts):
            pick = selector(places[s : s + 1])
            weight = jnp.sum(pick * weights[s], axis=1, keepdims=True)
            pick = pick.astype(bf16)
            for h in range(HALVES):
                side = jnp.bitwise_xor(at[0], h)
                cols = pl.ds(pl.multiple_of(side * span, span), span)
                out = outs[s].at[h]
                out[0] = jnp.dot(pick, t_ref[:, cols], preferred_element_type=f32).astype(bf16)
                out[1] = (
                    jnp.dot(pick, d_ref[:, cols], preferred_element_type=f32) * weight
                ).astype(bf16)

    *cut, places, weights = call(
        dispatch,
        [shape(HALVES, 2, CAP, span)] * experts + [shape(max(experts, 8), count, dtype=f32)] * 2,
        [here, routes.T, gate_scale.T, tokens, d_out],
    )
    *cut, own_c = lax.optimization_barrier((*cut, own_c))
    lead = [cut[0]] + [send(cut[s], shift=s) for s in range(1, experts)]
    follow = [send(m[1], half=1) for m in lead]
    pieces = [m[0] for m in lead] + follow

    *near, pieces[experts] = lax.optimization_barrier((*near, pieces[experts]))
    if two_hops:
        far = [send(near[0][0], chip=2), send(near[1][1], chip=1)]
    else:
        far = []
    *far, pieces = lax.optimization_barrier((*far, tuple(pieces)))
    here_blocks = [own] + near + far
    there_blocks = [own_c] + [send(m, core=1) for m in near + far]
    blocks = here_blocks + there_blocks

    def assemble(at, refs, held, kinds):
        for i, ref in enumerate(refs):
            core, place = divmod(i, len(here_blocks))
            for k in range(2):
                if len(ref.shape) == 4:
                    chip, part = place, ref.at[k]
                elif place - chips + 1 == k:
                    chip, part = chips - 1, ref
                else:
                    continue
                owner = jnp.bitwise_xor(at[1], chip) * CORES + jnp.bitwise_xor(at[2], core)
                start = pl.multiple_of(owner * block + k * half_block, half_block)
                for m, kind in enumerate(kinds):
                    held[m, pl.ds(start, half_block), :] = part[kind]

    def project(at, *refs):
        ins, refs = refs[: len(spots)], refs[len(spots) :]
        ws, (keep, give, held) = refs[: len(blocks)], refs[len(blocks) :]
        assemble(at, ws, held, (0, 1, 2))
        for m, side in enumerate((0, 0, 1)):
            left = jnp.concatenate([ref[side] for ref in ins], axis=0)
            part = jnp.dot(left, held[m], preferred_element_type=f32)
            keep[m] = part[:rows]
            give[m] = part[rows:].astype(bf16)

    keep, give = call(
        project,
        [shape(3, rows, inner, dtype=f32), shape(3, rows, inner)],
        [here, *pieces, *blocks],
        scratch=[pltpu.VMEM((3, span, inner), bf16)],
        flops=2 * 3 * HALVES * rows * span * inner,
    )
    came = send(give, half=1)

    def divide(at, *refs):
        ins, (stay, leave) = refs[: len(spots)], refs[len(spots) :]
        first = at[2] == 0
        for k in range(2):
            for i, ref in enumerate(ins):
                for chip in range(chips):
                    both = ref[k, :, chip * CORES * block : (chip + 1) * CORES * block]
                    low, high = both[:, :block], both[:, block:]
                    place = (k, slice(i * CAP, (i + 1) * CAP), slice(chip * block, (chip + 1) * block))
                    stay[place] = jnp.where(first, low, high)
                    leave[place] = jnp.where(first, high, low)

    stay, leave = call(
        divide, [shape(2, HALVES * rows, chips * block)] * 2, [here, *pieces]
    )
    across = send(leave, core=1)

    came, across = lax.optimization_barrier((came, across))

    def activate(at, keep_ref, came_ref, out):
        gate = keep_ref[0] + came_ref[0].astype(f32)
        up = keep_ref[1] + came_ref[1].astype(f32)
        d_hidden = keep_ref[2] + came_ref[2].astype(f32)
        sig = jax.nn.sigmoid(gate)
        act = gate * sig
        out[0] = (d_hidden * up * sig * (1.0 + gate * (1.0 - sig))).astype(bf16)
        out[1] = (d_hidden * act).astype(bf16)
        out[2] = (act * up).astype(bf16)

    (inside,) = call(activate, [shape(3, rows, inner)], [here, keep, came])
    other = send(inside, half=1)
    inside_c = send(inside, core=1)

    def weigh(at, a0, a1, a2, a3, x0, x1, *refs):
        outs, held = refs[:-1], refs[-1]
        for m in range(3):
            left = jnp.concatenate([x0[m // 2], x1[m // 2]], axis=0)
            right = jnp.concatenate([a0[m], a1[m], a2[m], a3[m]], axis=0)
            held[...] = lax.dot_general(left, right, CONTRACT_FIRST, preferred_element_type=f32)
            for o, out in enumerate(outs):
                start = pl.multiple_of(jnp.bitwise_xor(at[1], o) * block, block)
                out[m] = held[pl.ds(start, block), :].astype(out.dtype)

    other_c = send(other, core=1)

    def expand(at, a0, a1, *refs):
        ws, (*outs, held) = refs[: len(blocks)], refs[len(blocks) :]
        assemble(at, ws, held, (0, 1, 2))
        left = [jnp.concatenate([a0[m], a1[m]], axis=0) for m in range(3)]
        out = lax.dot_general(left[2], held[2], CONTRACT_LAST, preferred_element_type=f32)
        d_in = lax.dot_general(
            left[0], held[0], CONTRACT_LAST, preferred_element_type=f32
        ) + lax.dot_general(left[1], held[1], CONTRACT_LAST, preferred_element_type=f32)
        for s in range(experts):
            for h in range(HALVES):
                part = slice((h * experts + s) * CAP, (h * experts + s + 1) * CAP)
                ref = outs[s] if h == 0 else outs[experts].at[s]
                ref[0] = out[part].astype(bf16)
                ref[1] = d_in[part].astype(bf16)

    *back, far_back = call(
        expand,
        [shape(2, CAP, span)] * experts + [shape(experts, 2, CAP, span)],
        [here, inside, other, *blocks],
        scratch=[pltpu.VMEM((3, span, inner), bf16)],
        flops=2 * 3 * HALVES * rows * span * inner,
    )
    back, inside_c = lax.optimization_barrier((back, inside_c))
    grads = call(
        weigh,
        [shape(3, block, inner, dtype=f32)] + [shape(3, block, inner)] * (chips - 1),
        [here, inside, other, inside_c, other_c, stay, across],
        scratch=[pltpu.VMEM((chips * block, inner), f32)],
        flops=2 * 3 * CORES * HALVES * rows * chips * block * inner,
    )
    grads = [grads[0]] + [send(grads[o], chip=o) for o in range(1, chips)]
    far_back = send(far_back, half=1)
    home = [back[0]] + [send(back[s], shift=-s) for s in range(1, experts)]
    home += [far_back[0]] + [send(far_back[s], shift=-s) for s in range(1, experts)]

    def collect(at, p_ref, w_ref, *refs):
        ins, (out, d_in) = refs[: len(spots)], refs[len(spots) :]
        picks = [selector(p_ref[s : s + 1]).astype(bf16) for s in range(experts)]
        columns = jnp.transpose(w_ref[...])
        for h in range(HALVES):
            side = jnp.bitwise_xor(at[0], h)
            cols = pl.ds(pl.multiple_of(side * span, span), span)
            total_out = jnp.zeros((count, span), f32)
            total_in = jnp.zeros((count, span), f32)
            for s in range(experts):
                ref = ins[h * experts + s]
                total_out += columns[:, s : s + 1] * lax.dot_general(
                    picks[s], ref[0], CONTRACT_FIRST, preferred_element_type=f32
                )
                total_in += lax.dot_general(
                    picks[s], ref[1], CONTRACT_FIRST, preferred_element_type=f32
                )
            out[:, cols] = total_out.astype(bf16)
            d_in[:, cols] = total_in.astype(bf16)

    layer_out, d_tokens = call(
        collect, [shape(count, width)] * 2, [here, places, weights, *home]
    )

    d_tokens, grads = lax.optimization_barrier((d_tokens, grads))

    def finish(at, own, *refs):
        ins, outs = refs[: chips - 1], refs[chips - 1 :]
        for m, out in enumerate(outs):
            total = own[m]
            for ref in ins:
                total = total + ref[m].astype(f32)
            out[0] = total

    grad_gate, grad_up, grad_down = call(
        finish, [shape(1, block, inner, dtype=f32)] * 3, [here, *grads]
    )
    return layer_out, d_tokens, grad_gate, grad_up, grad_down


def solution(mesh):
    by_token = P(("dp", "expert"), None)
    by_expert = P("expert", "dp", None)
    return jax.shard_map(
        shards,
        mesh=mesh,
        in_specs=(by_token,) * 3 + (by_expert,) * 3 + (by_token,),
        out_specs=(by_token,) * 2 + (by_expert,) * 3,
        check_vma=False,
    )
```

time: 141 us -> 115 us (0.82)
  the two profiles are of different devices: /device:TPU:8 before, /device:TPU:0 now
where the time goes in v2:
time: 115 us
  waiting for transfers between devices  73.1 us (64%)
  starting transfers between devices  25.1 us (22%)
  Pallas kernels  14.7 us (13%)
  local copies, waits for them, and re-layouts  1.24 us (1%)
    ppermute x23, waiting for transfers between devices, send(): return lax.ppermute(value, ('dp', 'expert'), perm)  73.1 us
    ppermute x23, starting transfers between devices, send(): return lax.ppermute(value, ('dp', 'expert'), perm)  25.1 us
    pallas_call x8, Pallas kernels, call(): pl.pallas_call(kernel, out_shape=out_shape, in_specs=[pl.BlockSpec(memory...  12.6 us
  transfers between devices with their start and end apart: 23, of which 12 were waited for; matrix products, arithmetic and copies ran while one was open for 0% of the time, Pallas kernels for 8%

profile of v2, /device:TPU:0, one launch (start us, length us, event | category | flops | bytes accessed | tf_op | source)
XLA Modules:
  0.0 115.1 jit_solution(8911309076898484771)
XLA Ops:
  0.7 2.0 %shard_map.111.refs_4_.refs_0_ = bf16[2,3,64,768]{3,2,1,0:T(8,128)(2,1)} custom-call(bf16[1,128,768]{2,1,0:T(8,128)(2,1)} %g_ref.1, bf16[1,128,768]{2,1,0:T(8,128)(2,1)} %u_ref.1, bf16[1,128,768]{2,1,0:T(8,128)(2,1)} %w_ref.1), custom_call_target="tpu_custom_call" | custom-call | tf_op jit(solution)/shard_map/pallas_call | solution.py:87
  3.2 2.6 %collective-permute-start.1 = (bf16[2,3,64,768]{3,2,1,0:T(8,128)(2,1)}, bf16[2,3,64,768]{3,2,1,0:T(8,128)(2,1)S(1)}, u32[]{:S(2)}, u32[]{:S(2)}) collective-permute-start(bf16[2,3,64,768]{3,2,1,0:T(8,128)(2,1)} %shard_map.111.refs_4_.refs_0_), channel_id=1, source_target_pairs={{0,8},{1,9},{2,10},{3,11},{4,12},{5,13},{6,14},{7,15},{8,0},{9,1},... | collective-permute-start | bytes 1769480 | tf_op jit(solution)/shard_map/ppermute | solution.py:75
  5.7 1.5 %collective-permute-start = (bf16[2,3,64,768]{3,2,1,0:T(8,128)(2,1)}, bf16[2,3,64,768]{3,2,1,0:T(8,128)(2,1)S(1)}, u32[]{:S(2)}, u32[]{:S(2)}) collective-permute-start(bf16[2,3,64,768]{3,2,1,0:T(8,128)(2,1)} %shard_map.111.refs_4_.refs_0_), channel_id=1, source_target_pairs={{0,4},{1,5},{2,6},{3,7},{4,0},{5,1},{6,2},{7,3},{8,12},{9,13},{10,... | collective-permute-start | bytes 1769480 | tf_op jit(solution)/shard_map/ppermute | solution.py:75
  9.9 2.7 %collective-permute-start.3 = (bf16[2,32,1024]{2,1,0:T(8,128)(2,1)S(1)}, bf16[2,32,1024]{2,1,0:T(8,128)(2,1)S(1)}, u32[]{:S(2)}, u32[]{:S(2)}) collective-permute-start(bf16[2,32,1024]{2,1,0:T(8,128)(2,1)S(1)} %get-tuple-element.94), channel_id=1, source_target_pairs={{0,16},{1,17},{2,18},{3,19},{4,20},{5,21},{6,22},{7,23},{8,24},{9,... | collective-permute-start | bytes 393224 | tf_op jit(solution)/shard_map/ppermute | solution.py:75
  14.0 8.7 %collective-permute-done.1.refs_6_.refs_2_ = bf16[2,3,64,768]{3,2,1,0:T(8,128)(2,1)S(1)} collective-permute-done((bf16[2,3,64,768]{3,2,1,0:T(8,128)(2,1)}, bf16[2,3,64,768]{3,2,1,0:T(8,128)(2,1)S(1)}, u32[]{:S(2)}, u32[]{:S(2)}) %collective-permute-start.1) | collective-permute-done | bytes 589856 | tf_op jit(solution)/shard_map/ppermute | solution.py:75
  22.9 1.8 %collective-permute-start.5 = (bf16[3,64,768]{2,1,0:T(8,128)(2,1)S(1)}, bf16[3,64,768]{2,1,0:T(8,128)(2,1)S(1)}, u32[]{:S(2)}, u32[]{:S(2)}) collective-permute-start(bf16[3,64,768]{2,1,0:T(8,128)(2,1)S(1)} %slice_bitcast_fusion), channel_id=1, source_target_pairs={{0,4},{1,5},{2,6},{3,7},{4,0},{5,1},{6,2},{7,3},{8,12},{9,13},{10,... | collective-permute-start | bytes 884744 | tf_op jit(solution)/shard_map/ppermute | solution.py:75
  24.8 2.6 %collective-permute-start.4 = (bf16[3,64,768]{2,1,0:T(8,128)(2,1)S(1)}, bf16[3,64,768]{2,1,0:T(8,128)(2,1)S(1)}, u32[]{:S(2)}, u32[]{:S(2)}) collective-permute-start(bf16[3,64,768]{2,1,0:T(8,128)(2,1)S(1)} %slice_bitcast_fusion.1), channel_id=1, source_target_pairs={{0,8},{1,9},{2,10},{3,11},{4,12},{5,13},{6,14},{7,15},{8,0},{9,1},... | collective-permute-start | bytes 884744 | tf_op jit(solution)/shard_map/ppermute | solution.py:75
  27.5 1.6 %collective-permute-start.7 = (bf16[2,32,1024]{2,1,0:T(8,128)(2,1)S(1)}, bf16[2,32,1024]{2,1,0:T(8,128)(2,1)S(1)}, u32[]{:S(2)}, u32[]{:S(2)}) collective-permute-start(bf16[2,32,1024]{2,1,0:T(8,128)(2,1)S(1)} %get-tuple-element.91), channel_id=1, source_target_pairs={{0,16},{1,17},{2,18},{3,19},{4,20},{5,21},{6,22},{7,23},{8,24},{9,... | collective-permute-start | bytes 393224 | tf_op jit(solution)/shard_map/ppermute | solution.py:75
  29.1 7.9 %collective-permute-done.7.refs_3_ = bf16[2,32,1024]{2,1,0:T(8,128)(2,1)S(1)} collective-permute-done((bf16[2,32,1024]{2,1,0:T(8,128)(2,1)S(1)}, bf16[2,32,1024]{2,1,0:T(8,128)(2,1)S(1)}, u32[]{:S(2)}, u32[]{:S(2)}) %collective-permute-start.7) | collective-permute-done | bytes 131104 | tf_op jit(solution)/shard_map/ppermute | solution.py:75
  39.8 1.6 %shard_map.112 = (f32[3,64,768]{2,1,0:T(8,128)S(1)}, bf16[3,64,768]{2,1,0:T(8,128)(2,1)S(1)}) custom-call(s32[4]{0:T(128)S(1)} %pad_add_fusion.at, bf16[2,32,1024]{2,1,0:T(8,128)(2,1)S(1)} %get-tuple-element.56.refs_0_, bf16[2,32,1024]{2,1,0:T(8,128)(2,1)S(1)} %get-tuple-element.57.refs_1_, bf16[2,32,1024]{2,1,0:T(8,128)(2,1)S(1)} %collective-permute-done.3.refs_2_, ...), custom_call_target="tpu_custom_call" | custom-call | flops 603979776 | bytes 6127632 | tf_op jit(solution)/shard_map/pallas_call | solution.py:23
  41.4 2.7 %collective-permute-start.12 = (bf16[3,64,768]{2,1,0:T(8,128)(2,1)S(1)}, bf16[3,64,768]{2,1,0:T(8,128)(2,1)S(1)}, u32[]{:S(2)}, u32[]{:S(2)}) collective-permute-start(bf16[3,64,768]{2,1,0:T(8,128)(2,1)S(1)} %get-tuple-element.64), channel_id=1, source_target_pairs={{0,16},{1,17},{2,18},{3,19},{4,20},{5,21},{6,22},{7,23},{8,24},{9,... | collective-permute-start | bytes 884744 | tf_op jit(solution)/shard_map/ppermute | solution.py:75
  44.8 1.5 %collective-permute-done.13.x1 = bf16[2,128,512]{2,1,0:T(8,128)(2,1)S(1)} collective-permute-done((bf16[2,128,512]{2,1,0:T(8,128)(2,1)S(1)}, bf16[2,128,512]{2,1,0:T(8,128)(2,1)S(1)}, u32[]{:S(2)}, u32[]{:S(2)}) %collective-permute-start.13) | collective-permute-done | bytes 262176 | tf_op jit(solution)/shard_map/ppermute | solution.py:75
  46.4 11.4 %collective-permute-done.12.came_ref = bf16[3,64,768]{2,1,0:T(8,128)(2,1)S(1)} collective-permute-done((bf16[3,64,768]{2,1,0:T(8,128)(2,1)S(1)}, bf16[3,64,768]{2,1,0:T(8,128)(2,1)S(1)}, u32[]{:S(2)}, u32[]{:S(2)}) %collective-permute-start.12) | collective-permute-done | bytes 294944 | tf_op jit(solution)/shard_map/ppermute | solution.py:75
  58.6 15.4 %collective-permute-done.14.a1 = bf16[3,64,768]{2,1,0:T(8,128)(2,1)S(1)} collective-permute-done((bf16[3,64,768]{2,1,0:T(8,128)(2,1)S(1)}, bf16[3,64,768]{2,1,0:T(8,128)(2,1)S(1)}, u32[]{:S(2)}, u32[]{:S(2)}) %collective-permute-start.14) | collective-permute-done | bytes 294944 | tf_op jit(solution)/shard_map/ppermute | solution.py:75
  74.0 2.5 %shard_map.115 = (bf16[2,32,1024]{2,1,0:T(8,128)(2,1)S(1)}, bf16[2,32,1024]{2,1,0:T(8,128)(2,1)S(1)}, bf16[2,2,32,1024]{3,2,1,0:T(8,128)(2,1)S(1)}) custom-call(s32[4]{0:T(128)S(1)} %pad_add_fusion.at, bf16[3,64,768]{2,1,0:T(8,128)(2,1)S(1)} %shard_map.114.a0, bf16[3,64,768]{2,1,0:T(8,128)(2,1)S(1)} %collective-permute-done.14.a1, ...), custom_call_target="tpu_custom_call" | custom-call | flops 603979776 | bytes 5832720 | tf_op jit(solution)/shard_map/pallas_call | solution.py:23
  76.6 1.6 %shard_map.117 = (f32[3,128,768]{2,1,0:T(8,128)S(1)}, bf16[3,128,768]{2,1,0:T(8,128)(2,1)S(1)}, bf16[3,128,768]{2,1,0:T(8,128)(2,1)S(1)}, bf16[3,128,768]{2,1,0:T(8,128)(2,1)S(1)}) custom-call(s32[4]{0:T(128)S(1)} %pad_add_fusion.at, bf16[3,64,768]{2,1,0:T(8,128)(2,1)S(1)} %shard_map.114.a0, bf16[3,64,768]{2,1,0:T(8,128)(2,1)S(1)} %collective-permute-done.14.a1, ...), custom_call_target="tpu_custom_call" | custom-call | flops 603979776 | bytes 4653072 | tf_op jit(solution)/shard_map/pallas_call | solution.py:23
  78.8 1.7 %collective-permute-start.21 = (bf16[3,128,768]{2,1,0:T(8,128)(2,1)S(1)}, bf16[3,128,768]{2,1,0:T(8,128)(2,1)S(1)}, u32[]{:S(2)}, u32[]{:S(2)}) collective-permute-start(bf16[3,128,768]{2,1,0:T(8,128)(2,1)S(1)} %get-tuple-element.79), channel_id=1, source_target_pairs={{0,8},{1,9},{2,10},{3,11},{4,12},{5,13},{6,14},{7,15},{8,0},{9,1},... | collective-permute-start | bytes 1769480 | tf_op jit(solution)/shard_map/ppermute | solution.py:75
  83.3 7.1 %collective-permute-done.17 = bf16[2,2,32,1024]{3,2,1,0:T(8,128)(2,1)S(1)} collective-permute-done((bf16[2,2,32,1024]{3,2,1,0:T(8,128)(2,1)S(1)}, bf16[2,2,32,1024]{3,2,1,0:T(8,128)(2,1)S(1)}, u32[]{:S(2)}, u32[]{:S(2)}) %collective-permute-start.17) | collective-permute-done | bytes 262176 | tf_op jit(solution)/shard_map/ppermute | solution.py:75
  90.4 1.6 %collective-permute-start.18 = (bf16[2,32,1024]{2,1,0:T(8,128)(2,1)S(1)}, bf16[2,32,1024]{2,1,0:T(8,128)(2,1)S(1)}, u32[]{:S(2)}, u32[]{:S(2)}) collective-permute-start(bf16[2,32,1024]{2,1,0:T(8,128)(2,1)S(1)} %get-tuple-element.89), channel_id=1, source_target_pairs={{0,1},{1,0},{2,3},{3,2},{4,5},{5,4},{6,7},{7,6},{8,9},{9,8},{10,11... | collective-permute-start | bytes 393224 | tf_op jit(solution)/shard_map/ppermute | solution.py:75
  92.0 3.9 %collective-permute-done.18.refs_3_ = bf16[2,32,1024]{2,1,0:T(8,128)(2,1)S(1)} collective-permute-done((bf16[2,32,1024]{2,1,0:T(8,128)(2,1)S(1)}, bf16[2,32,1024]{2,1,0:T(8,128)(2,1)S(1)}, u32[]{:S(2)}, u32[]{:S(2)}) %collective-permute-start.18) | collective-permute-done | bytes 131104 | tf_op jit(solution)/shard_map/ppermute | solution.py:75
  95.9 2.5 %shard_map.116 = (bf16[192,2048]{1,0:T(8,128)(2,1)}, bf16[192,2048]{1,0:T(8,128)(2,1)}) custom-call(s32[4]{0:T(128)S(1)} %pad_add_fusion.at, f32[8,192]{1,0:T(8,128)S(1)} %get-tuple-element.47.p_ref, f32[8,192]{1,0:T(8,128)S(1)} %get-tuple-element.48.w_ref, bf16[2,32,1024]{2,1,0:T(8,128)(2,1)S(1)} %get-tuple-element.69.refs_0_, ...), custom_call_target="tpu_custom_call" | custom-call | bytes 2109456 | tf_op jit(solution)/shard_map/pallas_call | solution.py:23
  98.4 2.0 %collective-permute-done.21.refs_1_ = bf16[3,128,768]{2,1,0:T(8,128)(2,1)S(1)} collective-permute-done((bf16[3,128,768]{2,1,0:T(8,128)(2,1)S(1)}, bf16[3,128,768]{2,1,0:T(8,128)(2,1)S(1)}, u32[]{:S(2)}, u32[]{:S(2)}) %collective-permute-start.21) | collective-permute-done | bytes 589856 | tf_op jit(solution)/shard_map/ppermute | solution.py:75
  100.5 12.9 %collective-permute-done.22.refs_2_ = bf16[3,128,768]{2,1,0:T(8,128)(2,1)S(1)} collective-permute-done((bf16[3,128,768]{2,1,0:T(8,128)(2,1)S(1)}, bf16[3,128,768]{2,1,0:T(8,128)(2,1)S(1)}, u32[]{:S(2)}, u32[]{:S(2)}) %collective-permute-start.22) | collective-permute-done | bytes 589856 | tf_op jit(solution)/shard_map/ppermute | solution.py:75
  113.4 1.7 %shard_map.118 = (f32[1,128,768]{2,1,0:T(8,128)}, f32[1,128,768]{2,1,0:T(8,128)}, f32[1,128,768]{2,1,0:T(8,128)}) custom-call(s32[4]{0:T(128)S(1)} %pad_add_fusion.at, f32[3,128,768]{2,1,0:T(8,128)S(1)} %get-tuple-element.82.own, bf16[3,128,768]{2,1,0:T(8,128)(2,1)S(1)} %collective-permute-done.20.refs_0_, ...), custom_call_target="tpu_custom_call" | custom-call | bytes 4128784 | tf_op jit(solution)/shard_map/pallas_call | solution.py:23
  (47 shorter events, 12.5 us)
Async XLA Ops:
  2.7 7.2 %collective-permute-start.2 = (bf16[2,3,64,768]{3,2,1,0:T(8,128)(2,1)}, bf16[2,3,64,768]{3,2,1,0:T(8,128)(2,1)S(1)}, u32[]{:S(2)}, u32[]{:S(2)}) collective-permute-start(bf16[2,3,64,768]{3,2,1,0:T(8,128)(2,1)} %shard_map.111.refs_4_.refs_0_), channel_id=1, source_target_pairs={{0,2},{1,3},{2,0},{3,1},{4,6},{5,7},{6,4},{7,5},{8,10},{9,11},{10,... | collective-permute-start | bytes 1769480 | tf_op jit(solution)/shard_map/ppermute | solution.py:75
  3.2 19.6 %collective-permute-start.1 = (bf16[2,3,64,768]{3,2,1,0:T(8,128)(2,1)}, bf16[2,3,64,768]{3,2,1,0:T(8,128)(2,1)S(1)}, u32[]{:S(2)}, u32[]{:S(2)}) collective-permute-start(bf16[2,3,64,768]{3,2,1,0:T(8,128)(2,1)} %shard_map.111.refs_4_.refs_0_), channel_id=1, source_target_pairs={{0,8},{1,9},{2,10},{3,11},{4,12},{5,13},{6,14},{7,15},{8,0},{9,1},... | collective-permute-start | bytes 1769480 | tf_op jit(solution)/shard_map/ppermute | solution.py:75
  5.7 17.0 %collective-permute-start = (bf16[2,3,64,768]{3,2,1,0:T(8,128)(2,1)}, bf16[2,3,64,768]{3,2,1,0:T(8,128)(2,1)S(1)}, u32[]{:S(2)}, u32[]{:S(2)}) collective-permute-start(bf16[2,3,64,768]{3,2,1,0:T(8,128)(2,1)} %shard_map.111.refs_4_.refs_0_), channel_id=1, source_target_pairs={{0,4},{1,5},{2,6},{3,7},{4,0},{5,1},{6,2},{7,3},{8,12},{9,13},{10,... | collective-permute-start | bytes 1769480 | tf_op jit(solution)/shard_map/ppermute | solution.py:75
  9.9 29.9 %copy-start = (bf16[2,3,64,768]{3,2,1,0:T(8,128)(2,1)S(1)}, bf16[2,3,64,768]{3,2,1,0:T(8,128)(2,1)}, u32[]{:S(2)}) copy-start(bf16[2,3,64,768]{3,2,1,0:T(8,128)(2,1)} %shard_map.111.refs_4_.refs_0_) | copy-start | bytes 1769476
  9.9 12.9 %collective-permute-start.3 = (bf16[2,32,1024]{2,1,0:T(8,128)(2,1)S(1)}, bf16[2,32,1024]{2,1,0:T(8,128)(2,1)S(1)}, u32[]{:S(2)}, u32[]{:S(2)}) collective-permute-start(bf16[2,32,1024]{2,1,0:T(8,128)(2,1)S(1)} %get-tuple-element.94), channel_id=1, source_target_pairs={{0,16},{1,17},{2,18},{3,19},{4,20},{5,21},{6,22},{7,23},{8,24},{9,... | collective-permute-start | bytes 393224 | tf_op jit(solution)/shard_map/ppermute | solution.py:75
  12.6 14.9 %collective-permute-start.6 = (bf16[2,2,32,1024]{3,2,1,0:T(8,128)(2,1)S(1)}, bf16[2,2,32,1024]{3,2,1,0:T(8,128)(2,1)S(1)}, u32[]{:S(2)}, u32[]{:S(2)}) collective-permute-start(bf16[2,2,32,1024]{3,2,1,0:T(8,128)(2,1)S(1)} %get-tuple-element.54), channel_id=1, source_target_pairs={{0,1},{1,0},{2,3},{3,2},{4,5},{5,4},{6,7},{7,6},{8,9},{9,8},{10,11... | collective-permute-start | bytes 786440 | tf_op jit(solution)/shard_map/ppermute | solution.py:75
  22.8 15.5 %collective-permute-start.9 = (bf16[2,3,64,768]{3,2,1,0:T(8,128)(2,1)S(1)}, bf16[2,3,64,768]{3,2,1,0:T(8,128)(2,1)S(1)}, u32[]{:S(2)}, u32[]{:S(2)}) collective-permute-start(bf16[2,3,64,768]{3,2,1,0:T(8,128)(2,1)S(1)} %collective-permute-done.1.refs_6_.refs_2_), channel_id=1, source_target_pairs={{0,2},{1,3},{2,0},{3,1},{4,6},{5,7},{6,4},{7,5},{8,10},{9,11},{10,... | collective-permute-start | bytes 1769480 | tf_op jit(solution)/shard_map/ppermute | solution.py:75
  22.9 14.2 %collective-permute-start.5 = (bf16[3,64,768]{2,1,0:T(8,128)(2,1)S(1)}, bf16[3,64,768]{2,1,0:T(8,128)(2,1)S(1)}, u32[]{:S(2)}, u32[]{:S(2)}) collective-permute-start(bf16[3,64,768]{2,1,0:T(8,128)(2,1)S(1)} %slice_bitcast_fusion), channel_id=1, source_target_pairs={{0,4},{1,5},{2,6},{3,7},{4,0},{5,1},{6,2},{7,3},{8,12},{9,13},{10,... | collective-permute-start | bytes 884744 | tf_op jit(solution)/shard_map/ppermute | solution.py:75
  24.6 13.7 %collective-permute-start.8 = (bf16[2,3,64,768]{3,2,1,0:T(8,128)(2,1)S(1)}, bf16[2,3,64,768]{3,2,1,0:T(8,128)(2,1)S(1)}, u32[]{:S(2)}, u32[]{:S(2)}) collective-permute-start(bf16[2,3,64,768]{3,2,1,0:T(8,128)(2,1)S(1)} %collective-permute-done.refs_5_.refs_1_), channel_id=1, source_target_pairs={{0,2},{1,3},{2,0},{3,1},{4,6},{5,7},{6,4},{7,5},{8,10},{9,11},{10,... | collective-permute-start | bytes 1769480 | tf_op jit(solution)/shard_map/ppermute | solution.py:75
  24.8 13.0 %collective-permute-start.4 = (bf16[3,64,768]{2,1,0:T(8,128)(2,1)S(1)}, bf16[3,64,768]{2,1,0:T(8,128)(2,1)S(1)}, u32[]{:S(2)}, u32[]{:S(2)}) collective-permute-start(bf16[3,64,768]{2,1,0:T(8,128)(2,1)S(1)} %slice_bitcast_fusion.1), channel_id=1, source_target_pairs={{0,8},{1,9},{2,10},{3,11},{4,12},{5,13},{6,14},{7,15},{8,0},{9,1},... | collective-permute-start | bytes 884744 | tf_op jit(solution)/shard_map/ppermute | solution.py:75
  27.5 9.6 %collective-permute-start.7 = (bf16[2,32,1024]{2,1,0:T(8,128)(2,1)S(1)}, bf16[2,32,1024]{2,1,0:T(8,128)(2,1)S(1)}, u32[]{:S(2)}, u32[]{:S(2)}) collective-permute-start(bf16[2,32,1024]{2,1,0:T(8,128)(2,1)S(1)} %get-tuple-element.91), channel_id=1, source_target_pairs={{0,16},{1,17},{2,18},{3,19},{4,20},{5,21},{6,22},{7,23},{8,24},{9,... | collective-permute-start | bytes 393224 | tf_op jit(solution)/shard_map/ppermute | solution.py:75
  37.8 1.6 %collective-permute-start.10 = (bf16[3,64,768]{2,1,0:T(8,128)(2,1)S(1)}, bf16[3,64,768]{2,1,0:T(8,128)(2,1)S(1)}, u32[]{:S(2)}, u32[]{:S(2)}) collective-permute-start(bf16[3,64,768]{2,1,0:T(8,128)(2,1)S(1)} %collective-permute-done.4.refs_7_.refs_3_), channel_id=1, source_target_pairs={{0,2},{1,3},{2,0},{3,1},{4,6},{5,7},{6,4},{7,5},{8,10},{9,11},{10,... | collective-permute-start | bytes 884744 | tf_op jit(solution)/shard_map/ppermute | solution.py:75
  37.8 2.0 %collective-permute-start.11 = (bf16[3,64,768]{2,1,0:T(8,128)(2,1)S(1)}, bf16[3,64,768]{2,1,0:T(8,128)(2,1)S(1)}, u32[]{:S(2)}, u32[]{:S(2)}) collective-permute-start(bf16[3,64,768]{2,1,0:T(8,128)(2,1)S(1)} %collective-permute-done.5.refs_8_.refs_4_), channel_id=1, source_target_pairs={{0,2},{1,3},{2,0},{3,1},{4,6},{5,7},{6,4},{7,5},{8,10},{9,11},{10,... | collective-permute-start | bytes 884744 | tf_op jit(solution)/shard_map/ppermute | solution.py:75
  41.4 16.3 %collective-permute-start.12 = (bf16[3,64,768]{2,1,0:T(8,128)(2,1)S(1)}, bf16[3,64,768]{2,1,0:T(8,128)(2,1)S(1)}, u32[]{:S(2)}, u32[]{:S(2)}) collective-permute-start(bf16[3,64,768]{2,1,0:T(8,128)(2,1)S(1)} %get-tuple-element.64), channel_id=1, source_target_pairs={{0,16},{1,17},{2,18},{3,19},{4,20},{5,21},{6,22},{7,23},{8,24},{9,... | collective-permute-start | bytes 884744 | tf_op jit(solution)/shard_map/ppermute | solution.py:75
  44.8 1.6 %collective-permute-start.13 = (bf16[2,128,512]{2,1,0:T(8,128)(2,1)S(1)}, bf16[2,128,512]{2,1,0:T(8,128)(2,1)S(1)}, u32[]{:S(2)}, u32[]{:S(2)}) collective-permute-start(bf16[2,128,512]{2,1,0:T(8,128)(2,1)S(1)} %get-tuple-element.65), channel_id=1, source_target_pairs={{0,2},{1,3},{2,0},{3,1},{4,6},{5,7},{6,4},{7,5},{8,10},{9,11},{10,... | collective-permute-start | bytes 786440 | tf_op jit(solution)/shard_map/ppermute | solution.py:75
  58.4 15.5 %collective-permute-start.14 = (bf16[3,64,768]{2,1,0:T(8,128)(2,1)S(1)}, bf16[3,64,768]{2,1,0:T(8,128)(2,1)S(1)}, u32[]{:S(2)}, u32[]{:S(2)}) collective-permute-start(bf16[3,64,768]{2,1,0:T(8,128)(2,1)S(1)} %shard_map.114.a0), channel_id=1, source_target_pairs={{0,16},{1,17},{2,18},{3,19},{4,20},{5,21},{6,22},{7,23},{8,24},{9,... | collective-permute-start | bytes 884744 | tf_op jit(solution)/shard_map/ppermute | solution.py:75
  58.5 17.9 %collective-permute-start.15 = (bf16[3,64,768]{2,1,0:T(8,128)(2,1)S(1)}, bf16[3,64,768]{2,1,0:T(8,128)(2,1)S(1)}, u32[]{:S(2)}, u32[]{:S(2)}) collective-permute-start(bf16[3,64,768]{2,1,0:T(8,128)(2,1)S(1)} %shard_map.114.a0), channel_id=1, source_target_pairs={{0,2},{1,3},{2,0},{3,1},{4,6},{5,7},{6,4},{7,5},{8,10},{9,11},{10,... | collective-permute-start | bytes 884744 | tf_op jit(solution)/shard_map/ppermute | solution.py:75
  74.0 2.6 %collective-permute-start.19 = (bf16[3,64,768]{2,1,0:T(8,128)(2,1)S(1)}, bf16[3,64,768]{2,1,0:T(8,128)(2,1)S(1)}, u32[]{:S(2)}, u32[]{:S(2)}) collective-permute-start(bf16[3,64,768]{2,1,0:T(8,128)(2,1)S(1)} %collective-permute-done.14.a1), channel_id=1, source_target_pairs={{0,2},{1,3},{2,0},{3,1},{4,6},{5,7},{6,4},{7,5},{8,10},{9,11},{10,... | collective-permute-start | bytes 884744 | tf_op jit(solution)/shard_map/ppermute | solution.py:75
  76.5 13.9 %collective-permute-start.17 = (bf16[2,2,32,1024]{3,2,1,0:T(8,128)(2,1)S(1)}, bf16[2,2,32,1024]{3,2,1,0:T(8,128)(2,1)S(1)}, u32[]{:S(2)}, u32[]{:S(2)}) collective-permute-start(bf16[2,2,32,1024]{3,2,1,0:T(8,128)(2,1)S(1)} %get-tuple-element.71), channel_id=1, source_target_pairs={{0,16},{1,17},{2,18},{3,19},{4,20},{5,21},{6,22},{7,23},{8,24},{9,... | collective-permute-start | bytes 786440 | tf_op jit(solution)/shard_map/ppermute | solution.py:75
  78.2 20.2 %collective-permute-start.20 = (bf16[3,128,768]{2,1,0:T(8,128)(2,1)S(1)}, bf16[3,128,768]{2,1,0:T(8,128)(2,1)S(1)}, u32[]{:S(2)}, u32[]{:S(2)}) collective-permute-start(bf16[3,128,768]{2,1,0:T(8,128)(2,1)S(1)} %get-tuple-element.78), channel_id=1, source_target_pairs={{0,4},{1,5},{2,6},{3,7},{4,0},{5,1},{6,2},{7,3},{8,12},{9,13},{10,... | collective-permute-start | bytes 1769480 | tf_op jit(solution)/shard_map/ppermute | solution.py:75
  78.8 21.7 %collective-permute-start.21 = (bf16[3,128,768]{2,1,0:T(8,128)(2,1)S(1)}, bf16[3,128,768]{2,1,0:T(8,128)(2,1)S(1)}, u32[]{:S(2)}, u32[]{:S(2)}) collective-permute-start(bf16[3,128,768]{2,1,0:T(8,128)(2,1)S(1)} %get-tuple-element.79), channel_id=1, source_target_pairs={{0,8},{1,9},{2,10},{3,11},{4,12},{5,13},{6,14},{7,15},{8,0},{9,1},... | collective-permute-start | bytes 1769480 | tf_op jit(solution)/shard_map/ppermute | solution.py:75
  80.5 32.8 %collective-permute-start.22 = (bf16[3,128,768]{2,1,0:T(8,128)(2,1)S(1)}, bf16[3,128,768]{2,1,0:T(8,128)(2,1)S(1)}, u32[]{:S(2)}, u32[]{:S(2)}) collective-permute-start(bf16[3,128,768]{2,1,0:T(8,128)(2,1)S(1)} %get-tuple-element.80), channel_id=1, source_target_pairs={{0,12},{1,13},{2,14},{3,15},{4,8},{5,9},{6,10},{7,11},{8,4},{9,5},... | collective-permute-start | bytes 1769480 | tf_op jit(solution)/shard_map/ppermute | solution.py:75
  81.8 10.2 %collective-permute-start.16 = (bf16[2,32,1024]{2,1,0:T(8,128)(2,1)S(1)}, bf16[2,32,1024]{2,1,0:T(8,128)(2,1)S(1)}, u32[]{:S(2)}, u32[]{:S(2)}) collective-permute-start(bf16[2,32,1024]{2,1,0:T(8,128)(2,1)S(1)} %get-tuple-element.70), channel_id=1, source_target_pairs={{0,1},{1,0},{2,3},{3,2},{4,5},{5,4},{6,7},{7,6},{8,9},{9,8},{10,11... | collective-permute-start | bytes 393224 | tf_op jit(solution)/shard_map/ppermute | solution.py:75
  90.4 5.5 %collective-permute-start.18 = (bf16[2,32,1024]{2,1,0:T(8,128)(2,1)S(1)}, bf16[2,32,1024]{2,1,0:T(8,128)(2,1)S(1)}, u32[]{:S(2)}, u32[]{:S(2)}) collective-permute-start(bf16[2,32,1024]{2,1,0:T(8,128)(2,1)S(1)} %get-tuple-element.89), channel_id=1, source_target_pairs={{0,1},{1,0},{2,3},{3,2},{4,5},{5,4},{6,7},{7,6},{8,9},{9,8},{10,11... | collective-permute-start | bytes 393224 | tf_op jit(solution)/shard_map/ppermute | solution.py:75
  (4 other events, 21.2 us)

commit v3 on v2

--- a/solution.py
+++ b/solution.py
@@ -10,21 +10,24 @@
 CAP = 32
 CORES = 2
 HALVES = 2
+PARTS = 2
 VMEM_BYTES = 48 * 1024 * 1024
 
 CONTRACT_LAST = (((1,), (1,)), ((), ()))
 CONTRACT_FIRST = (((0,), (0,)), ((), ()))
 
 
-def call(kernel, out_shape, args, scratch=(), flops=0):
+def call(kernel, out_shape, args, scratch=(), flops=0, positions=True):
     moved = sum(a.size * a.dtype.itemsize for a in args) + sum(
         o.size * o.dtype.itemsize for o in out_shape
     )
     return pl.pallas_call(
         kernel,
         out_shape=out_shape,
-        in_specs=[pl.BlockSpec(memory_space=pltpu.SMEM)]
-        + [pl.BlockSpec(memory_space=pltpu.VMEM)] * (len(args) - 1),
+        in_specs=[
+            pl.BlockSpec(memory_space=pltpu.SMEM if positions and i == 0 else pltpu.VMEM)
+            for i in range(len(args))
+        ],
         out_specs=[pl.BlockSpec(memory_space=pltpu.VMEM)] * len(out_shape),
         scratch_shapes=list(scratch),
         compiler_params=pltpu.CompilerParams(vmem_limit_bytes=VMEM_BYTES),
@@ -78,16 +81,31 @@
         return jax.ShapeDtypeStruct(dims, dtype)
 
     half_block = block // 2
-
-    def pack(g_ref, u_ref, w_ref, out):
+    strip = inner // PARTS
+    two_hops = chips == 4
+
+    def pack(g_ref, u_ref, w_ref, *outs):
         for m, ref in enumerate((g_ref, u_ref, w_ref)):
             for k in range(2):
-                out[k, m] = ref[0, k * half_block : (k + 1) * half_block]
-
-    own = pl.pallas_call(pack, out_shape=shape(2, 3, half_block, inner))(w_gate, w_up, w_down)
-    two_hops = chips == 4
-    near = [send(own, chip=o) for o in range(1, chips - 1 if two_hops else chips)]
-    own_c = send(own, core=1)
+                for i, out in enumerate(outs):
+                    out[k, m] = ref[
+                        0, k * half_block : (k + 1) * half_block, i * strip : (i + 1) * strip
+                    ]
+
+    owns = list(
+        pl.pallas_call(pack, out_shape=[shape(2, 3, half_block, strip)] * PARTS)(
+            w_gate, w_up, w_down
+        )
+    )
+
+    def first_hop(own):
+        return [send(own, chip=o) for o in range(1, chips - 1 if two_hops else chips)]
+
+    def second_hop(near):
+        return [send(near[0][0], chip=2), send(near[1][1], chip=1)] if two_hops else []
+
+    near = first_hop(owns[0])
+    own_c = send(owns[0], core=1)
 
     def dispatch(at, r_ref, s_ref, t_ref, d_ref, *outs):
         *outs, p_ref, c_ref = outs
@@ -127,18 +145,19 @@
     pieces = [m[0] for m in lead] + follow
 
     *near, pieces[experts] = lax.optimization_barrier((*near, pieces[experts]))
-    if two_hops:
-        far = [send(near[0][0], chip=2), send(near[1][1], chip=1)]
-    else:
-        far = []
-    *far, pieces = lax.optimization_barrier((*far, tuple(pieces)))
-    here_blocks = [own] + near + far
-    there_blocks = [own_c] + [send(m, core=1) for m in near + far]
-    blocks = here_blocks + there_blocks
-
-    def assemble(at, refs, held, kinds):
+    far = second_hop(near)
+    reach = len(owns[:1]) + len(near) + len(far)
+    parts = [[owns[0], *near, *far, own_c] + [send(m, core=1) for m in near + far]]
+    for i in range(1, PARTS):
+        owns[i], far = lax.optimization_barrier((owns[i], far or near[-1:]))
+        near = first_hop(owns[i])
+        far = second_hop(near)
+        mine = [owns[i], *near, *far]
+        parts.append(mine + [send(m, core=1) for m in mine])
+
+    def assemble(at, refs, held, column):
         for i, ref in enumerate(refs):
-            core, place = divmod(i, len(here_blocks))
+            core, place = divmod(i, reach)
             for k in range(2):
                 if len(ref.shape) == 4:
                     chip, part = place, ref.at[k]
@@ -148,27 +167,32 @@
                     continue
                 owner = jnp.bitwise_xor(at[1], chip) * CORES + jnp.bitwise_xor(at[2], core)
                 start = pl.multiple_of(owner * block + k * half_block, half_block)
-                for m, kind in enumerate(kinds):
-                    held[m, pl.ds(start, half_block), :] = part[kind]
+                for m in range(3):
+                    held[m, pl.ds(start, half_block), column : column + strip] = part[m]
 
     def project(at, *refs):
         ins, refs = refs[: len(spots)], refs[len(spots) :]
-        ws, (keep, give, held) = refs[: len(blocks)], refs[len(blocks) :]
-        assemble(at, ws, held, (0, 1, 2))
+        *ws, keep, give, held = refs
+        assemble(at, ws, held, 0)
         for m, side in enumerate((0, 0, 1)):
             left = jnp.concatenate([ref[side] for ref in ins], axis=0)
             part = jnp.dot(left, held[m], preferred_element_type=f32)
-            keep[m] = part[:rows]
-            give[m] = part[rows:].astype(bf16)
-
-    keep, give = call(
-        project,
-        [shape(3, rows, inner, dtype=f32), shape(3, rows, inner)],
-        [here, *pieces, *blocks],
-        scratch=[pltpu.VMEM((3, span, inner), bf16)],
-        flops=2 * 3 * HALVES * rows * span * inner,
-    )
-    came = send(give, half=1)
+            keep[m] = part
+            give[m, :rows] = part[rows:].astype(bf16)
+            give[m, rows:] = part[:rows].astype(bf16)
+
+    keeps, gives = [], []
+    for i in range(PARTS):
+        keep, give = call(
+            project,
+            [shape(3, HALVES * rows, strip, dtype=f32), shape(3, HALVES * rows, strip)],
+            [here, *pieces, *parts[i]],
+            scratch=[pltpu.VMEM((3, span, strip), bf16)],
+            flops=2 * 3 * HALVES * rows * span * strip,
+        )
+        keeps.append(keep)
+        gives.append(give)
+    cames = [send(gives[0], half=1)]
 
     def divide(at, *refs):
         ins, (stay, leave) = refs[: len(spots)], refs[len(spots) :]
@@ -182,12 +206,15 @@
                     stay[place] = jnp.where(first, low, high)
                     leave[place] = jnp.where(first, high, low)
 
+    keeps[0], apart = lax.optimization_barrier((keeps[0], tuple(pieces)))
     stay, leave = call(
-        divide, [shape(2, HALVES * rows, chips * block)] * 2, [here, *pieces]
+        divide, [shape(2, HALVES * rows, chips * block)] * 2, [here, *apart]
     )
     across = send(leave, core=1)
 
-    came, across = lax.optimization_barrier((came, across))
+    cames[0], across = lax.optimization_barrier((cames[0], across))
+    for i in range(1, PARTS):
+        cames.append(send(gives[i], half=1))
 
     def activate(at, keep_ref, came_ref, out):
         gate = keep_ref[0] + came_ref[0].astype(f32)
@@ -199,26 +226,88 @@
         out[1] = (d_hidden * act).astype(bf16)
         out[2] = (act * up).astype(bf16)
 
-    (inside,) = call(activate, [shape(3, rows, inner)], [here, keep, came])
-    other = send(inside, half=1)
-    inside_c = send(inside, core=1)
-
-    def weigh(at, a0, a1, a2, a3, x0, x1, *refs):
+    low, high = slice(0, half_block), slice(half_block, block)
+
+    def weigh(at, mine, theirs, x0, x1, *refs):
         outs, held = refs[:-1], refs[-1]
         for m in range(3):
             left = jnp.concatenate([x0[m // 2], x1[m // 2]], axis=0)
-            right = jnp.concatenate([a0[m], a1[m], a2[m], a3[m]], axis=0)
+            right = jnp.concatenate([mine[m], theirs[m]], axis=0)
             held[...] = lax.dot_general(left, right, CONTRACT_FIRST, preferred_element_type=f32)
-            for o, out in enumerate(outs):
+
+            def owned(o):
                 start = pl.multiple_of(jnp.bitwise_xor(at[1], o) * block, block)
-                out[m] = held[pl.ds(start, block), :].astype(out.dtype)
-
-    other_c = send(other, core=1)
-
-    def expand(at, a0, a1, *refs):
-        ws, (*outs, held) = refs[: len(blocks)], refs[len(blocks) :]
-        assemble(at, ws, held, (0, 1, 2))
-        left = [jnp.concatenate([a0[m], a1[m]], axis=0) for m in range(3)]
+                return held[pl.ds(start, block), :]
+
+            outs[0][m] = owned(0)
+            if two_hops:
+                _, by_first, by_second, kept = outs
+                first, second, across_it = owned(1), owned(2), owned(3)
+                by_first[0, m] = across_it[low].astype(bf16)
+                by_first[1, m] = first[low].astype(bf16)
+                by_second[0, m] = across_it[high].astype(bf16)
+                by_second[1, m] = second[high].astype(bf16)
+                kept[0, m] = second[low]
+                kept[1, m] = first[high]
+            else:
+                for o in range(1, chips):
+                    outs[o][m] = owned(o).astype(bf16)
+
+    def weigh_with(mine, theirs):
+        if two_hops:
+            others = [shape(2, 3, half_block, strip)] * 2
+            others.append(shape(2, 3, half_block, strip, dtype=f32))
+        else:
+            others = [shape(3, block, strip)] * (chips - 1)
+        return list(
+            call(
+                weigh,
+                [shape(3, block, strip, dtype=f32), *others],
+                [here, mine, theirs, stay, across],
+                scratch=[pltpu.VMEM((chips * block, strip), f32)],
+                flops=2 * 3 * CORES * HALVES * rows * chips * block * strip,
+            )
+        )
+
+    def relay(kept, from_first, from_second, to_second, to_first):
+        to_second[...] = (kept[0] + from_first[0].astype(f32)).astype(bf16)
+        to_first[...] = (kept[1] + from_second[0].astype(f32)).astype(bf16)
+
+    def leave_first(grads):
+        if two_hops:
+            return [send(grads[1], chip=1), send(grads[2], chip=2)]
+        return [send(grads[o], chip=o) for o in range(1, chips)]
+
+    def join(grads, came):
+        if not two_hops:
+            return []
+        return list(
+            call(relay, [shape(3, half_block, strip)] * 2, [grads[3], *came], positions=False)
+        )
+
+    def leave_second(joined):
+        return [send(m, chip=2 - i) for i, m in enumerate(joined)]
+
+    inside, inside_c, arrived = [], [], []
+    for i in range(PARTS):
+        inside += call(
+            activate, [shape(3, HALVES * rows, strip)], [here, keeps[i], cames[i]]
+        )
+        inside_c.append(send(inside[i], core=1))
+        if i + 1 < PARTS:
+            grads = weigh_with(inside[i], inside_c[i])
+            grads[0], cames[i + 1] = lax.optimization_barrier((grads[0], cames[i + 1]))
+            hop = leave_first(grads)
+            hop[0], cames[i + 1] = lax.optimization_barrier((hop[0], cames[i + 1]))
+            joined = join(grads, hop)
+            arrived.append([grads[0], *hop, *leave_second(joined)])
+
+    def expand(at, *refs):
+        count_outs = HALVES * experts + 1
+        ins, ws, (*outs, held) = refs[:PARTS], refs[PARTS:-count_outs], refs[-count_outs:]
+        for i in range(PARTS):
+            assemble(at, ws[i * len(parts[0]) : (i + 1) * len(parts[0])], held, i * strip)
+        left = [jnp.concatenate([ref[m] for ref in ins], axis=1) for m in range(3)]
         out = lax.dot_general(left[2], held[2], CONTRACT_LAST, preferred_element_type=f32)
         d_in = lax.dot_general(
             left[0], held[0], CONTRACT_LAST, preferred_element_type=f32
@@ -226,29 +315,30 @@
         for s in range(experts):
             for h in range(HALVES):
                 part = slice((h * experts + s) * CAP, (h * experts + s + 1) * CAP)
-                ref = outs[s] if h == 0 else outs[experts].at[s]
+                ref = outs[h * experts + s]
                 ref[0] = out[part].astype(bf16)
                 ref[1] = d_in[part].astype(bf16)
 
-    *back, far_back = call(
+    back = call(
         expand,
-        [shape(2, CAP, span)] * experts + [shape(experts, 2, CAP, span)],
-        [here, inside, other, *blocks],
+        [shape(2, CAP, span)] * len(spots),
+        [here, *inside, *sum(parts, [])],
         scratch=[pltpu.VMEM((3, span, inner), bf16)],
         flops=2 * 3 * HALVES * rows * span * inner,
     )
-    back, inside_c = lax.optimization_barrier((back, inside_c))
-    grads = call(
-        weigh,
-        [shape(3, block, inner, dtype=f32)] + [shape(3, block, inner)] * (chips - 1),
-        [here, inside, other, inside_c, other_c, stay, across],
-        scratch=[pltpu.VMEM((chips * block, inner), f32)],
-        flops=2 * 3 * CORES * HALVES * rows * chips * block * inner,
-    )
-    grads = [grads[0]] + [send(grads[o], chip=o) for o in range(1, chips)]
-    far_back = send(far_back, half=1)
-    home = [back[0]] + [send(back[s], shift=-s) for s in range(1, experts)]
-    home += [far_back[0]] + [send(far_back[s], shift=-s) for s in range(1, experts)]
+    *back, inside_c[-1] = lax.optimization_barrier((*back, inside_c[-1]))
+    last = weigh_with(inside[-1], inside_c[-1])
+    hop = leave_first(last)
+    joined = join(last, hop)
+    home = {(0, 0): back[0]}
+    for i, (h, s) in enumerate(spots):
+        if h > 0:
+            home[h, s] = send(back[i], half=h, shift=-s)
+    joined, near_back = lax.optimization_barrier((joined, tuple(back[1:experts])))
+    for s in range(1, experts):
+        home[0, s] = send(near_back[s - 1], shift=-s)
+    home = [home[spot] for spot in spots]
+    arrived.append([last[0], *hop, *leave_second(joined)])
 
     def collect(at, p_ref, w_ref, *refs):
         ins, (out, d_in) = refs[: len(spots)], refs[len(spots) :]
@@ -274,18 +364,30 @@
         collect, [shape(count, width)] * 2, [here, places, weights, *home]
     )
 
-    d_tokens, grads = lax.optimization_barrier((d_tokens, grads))
-
-    def finish(at, own, *refs):
-        ins, outs = refs[: chips - 1], refs[chips - 1 :]
-        for m, out in enumerate(outs):
-            total = own[m]
-            for ref in ins:
-                total = total + ref[m].astype(f32)
-            out[0] = total
+    d_tokens, arrived = lax.optimization_barrier((d_tokens, arrived))
+
+    def finish(*refs):
+        group = len(arrived[0])
+        for i in range(PARTS):
+            mine, *ins = refs[i * group : (i + 1) * group]
+            cols = slice(i * strip, (i + 1) * strip)
+            for m, out in enumerate(refs[PARTS * group :]):
+                if two_hops:
+                    from_first, from_second, last_second, last_first = ins
+                    out[0, low, cols] = (
+                        mine[m, low] + from_first[1, m].astype(f32) + last_second[m].astype(f32)
+                    )
+                    out[0, high, cols] = (
+                        mine[m, high] + from_second[1, m].astype(f32) + last_first[m].astype(f32)
+                    )
+                else:
+                    total = mine[m]
+                    for ref in ins:
+                        total = total + ref[m].astype(f32)
+                    out[0, :, cols] = total
 
     grad_gate, grad_up, grad_down = call(
-        finish, [shape(1, block, inner, dtype=f32)] * 3, [here, *grads]
+        finish, [shape(1, block, inner, dtype=f32)] * 3, sum(arrived, []), positions=False
     )
     return layer_out, d_tokens, grad_gate, grad_up, grad_down
 

time: 115 us -> 105 us (0.913)
  waiting for transfers between devices: 73.1 us -> 49.7 us
  starting transfers between devices: 25.1 us -> 33.9 us
  Pallas kernels: 14.7 us -> 16.8 us
  local copies, waits for them, and re-layouts: 1.24 us -> 3.02 us
    ppermute x23 -> x37, waiting for transfers between devices: 73.1 us -> 49.7 us  [send(): return lax.ppermute(value, ('dp', 'expert'), perm)]
    ppermute x23 -> x37, starting transfers between devices: 25.1 us -> 33.9 us  [send(): return lax.ppermute(value, ('dp', 'expert'), perm)]
    pallas_call x8 -> x13, Pallas kernels: 12.6 us -> 14.9 us  [call(): pl.pallas_call(kernel, out_shape=out_shape, in_specs=[pl.BlockSpec(memory...]
    unnamed x10 -> x12, local copies, waits for them, and re-layouts: 1.14 us -> 2.91 us
  transfers between devices with their start and end apart: 23 -> 37, of which waited for: 12 -> 13; matrix products, arithmetic and copies ran while one was open for 0% -> 0% of each run, Pallas kernels for 8% -> 12%
where the time goes in v3:
time: 105 us; the launch traced here: 104 us
  waiting for transfers between devices  49.7 us (47%)
  starting transfers between devices  33.9 us (32%)
  Pallas kernels  16.8 us (16%)
  local copies, waits for them, and re-layouts  3.02 us (3%)
    ppermute x37, waiting for transfers between devices, send(): return lax.ppermute(value, ('dp', 'expert'), perm)  49.7 us
    ppermute x37, starting transfers between devices, send(): return lax.ppermute(value, ('dp', 'expert'), perm)  33.9 us
    pallas_call x13, Pallas kernels, call(): pl.pallas_call(kernel, out_shape=out_shape, in_specs=[pl.BlockSpec(memory...  14.9 us
    unnamed x12, local copies, waits for them, and re-layouts  2.91 us
  transfers between devices with their start and end apart: 37, of which 13 were waited for; matrix products, arithmetic and copies ran while one was open for 0% of the time, Pallas kernels for 12%

profile of v3, /device:TPU:0, one launch (start us, length us, event | category | flops | bytes accessed | tf_op | source)
XLA Modules:
  0.0 104.4 jit_solution(16862653255557075109)
XLA Ops:
  0.6 2.0 %shard_map.111 = (bf16[2,3,64,384]{3,2,1,0:T(8,128)(2,1)}, bf16[2,3,64,384]{3,2,1,0:T(8,128)(2,1)}) custom-call(bf16[1,128,768]{2,1,0:T(8,128)(2,1)} %g_ref.1, bf16[1,128,768]{2,1,0:T(8,128)(2,1)} %u_ref.1, bf16[1,128,768]{2,1,0:T(8,128)(2,1)} %w_ref.1), custom_call_target="tpu_custom_call" | custom-call | tf_op jit(solution)/shard_map/pallas_call | solution.py:96
  3.1 2.6 %collective-permute-start.3 = (bf16[2,3,64,384]{3,2,1,0:T(8,128)(2,1)}, bf16[2,3,64,384]{3,2,1,0:T(8,128)(2,1)S(1)}, u32[]{:S(2)}, u32[]{:S(2)}) collective-permute-start(bf16[2,3,64,384]{3,2,1,0:T(8,128)(2,1)} %get-tuple-element.79.refs_4_.refs_2_), channel_id=1, source_target_pairs={{0,8},{1,9},{2,10},{3,11},{4,12},{5,13},{6,14},{7,15},{8,0},{9,1},... | collective-permute-start | bytes 884744 | tf_op jit(solution)/shard_map/ppermute | solution.py:78
  5.6 1.5 %collective-permute-start.2 = (bf16[2,3,64,384]{3,2,1,0:T(8,128)(2,1)}, bf16[2,3,64,384]{3,2,1,0:T(8,128)(2,1)S(1)}, u32[]{:S(2)}, u32[]{:S(2)}) collective-permute-start(bf16[2,3,64,384]{3,2,1,0:T(8,128)(2,1)} %get-tuple-element.79.refs_4_.refs_2_), channel_id=1, source_target_pairs={{0,4},{1,5},{2,6},{3,7},{4,0},{5,1},{6,2},{7,3},{8,12},{9,13},{10,... | collective-permute-start | bytes 884744 | tf_op jit(solution)/shard_map/ppermute | solution.py:78
  11.6 2.7 %collective-permute-start.4 = (bf16[2,32,1024]{2,1,0:T(8,128)(2,1)S(1)}, bf16[2,32,1024]{2,1,0:T(8,128)(2,1)S(1)}, u32[]{:S(2)}, u32[]{:S(2)}) collective-permute-start(bf16[2,32,1024]{2,1,0:T(8,128)(2,1)S(1)} %get-tuple-element.147), channel_id=1, source_target_pairs={{0,16},{1,17},{2,18},{3,19},{4,20},{5,21},{6,22},{7,23},{8,24},{9,... | collective-permute-start | bytes 393224 | tf_op jit(solution)/shard_map/ppermute | solution.py:78
  14.2 1.5 %collective-permute-start.1 = (bf16[2,2,32,1024]{3,2,1,0:T(8,128)(2,1)S(1)}, bf16[2,2,32,1024]{3,2,1,0:T(8,128)(2,1)S(1)}, u32[]{:S(2)}, u32[]{:S(2)}) collective-permute-start(bf16[2,2,32,1024]{3,2,1,0:T(8,128)(2,1)S(1)} %get-tuple-element.81), channel_id=1, source_target_pairs={{0,1},{1,0},{2,3},{3,2},{4,5},{5,4},{6,7},{7,6},{8,9},{9,8},{10,11... | collective-permute-start | bytes 786440 | tf_op jit(solution)/shard_map/ppermute | solution.py:78
  15.7 5.0 %collective-permute-done.4.refs_2_ = bf16[2,32,1024]{2,1,0:T(8,128)(2,1)S(1)} collective-permute-done((bf16[2,32,1024]{2,1,0:T(8,128)(2,1)S(1)}, bf16[2,32,1024]{2,1,0:T(8,128)(2,1)S(1)}, u32[]{:S(2)}, u32[]{:S(2)}) %collective-permute-start.4) | collective-permute-done | bytes 131104 | tf_op jit(solution)/shard_map/ppermute | solution.py:78
  22.1 2.7 %collective-permute-start.5 = (bf16[2,32,1024]{2,1,0:T(8,128)(2,1)S(1)}, bf16[2,32,1024]{2,1,0:T(8,128)(2,1)S(1)}, u32[]{:S(2)}, u32[]{:S(2)}) collective-permute-start(bf16[2,32,1024]{2,1,0:T(8,128)(2,1)S(1)} %get-tuple-element.145), channel_id=1, source_target_pairs={{0,16},{1,17},{2,18},{3,19},{4,20},{5,21},{6,22},{7,23},{8,24},{9,... | collective-permute-start | bytes 393224 | tf_op jit(solution)/shard_map/ppermute | solution.py:78
  24.8 2.3 %collective-permute-done.7.refs_8_.refs_6_ = bf16[3,64,384]{2,1,0:T(8,128)(2,1)S(1)} collective-permute-done((bf16[3,64,384]{2,1,0:T(8,128)(2,1)S(1)}, bf16[3,64,384]{2,1,0:T(8,128)(2,1)S(1)}, u32[]{:S(2)}, u32[]{:S(2)}) %collective-permute-start.7) | collective-permute-done | bytes 147488 | tf_op jit(solution)/shard_map/ppermute | solution.py:78
  27.0 3.5 %collective-permute-done.6.refs_7_.refs_5_ = bf16[3,64,384]{2,1,0:T(8,128)(2,1)S(1)} collective-permute-done((bf16[3,64,384]{2,1,0:T(8,128)(2,1)S(1)}, bf16[3,64,384]{2,1,0:T(8,128)(2,1)S(1)}, u32[]{:S(2)}, u32[]{:S(2)}) %collective-permute-start.6) | collective-permute-done | bytes 147488 | tf_op jit(solution)/shard_map/ppermute | solution.py:78
  31.9 1.5 %collective-permute-start.14 = (bf16[2,3,64,384]{3,2,1,0:T(8,128)(2,1)S(1)}, bf16[2,3,64,384]{3,2,1,0:T(8,128)(2,1)S(1)}, u32[]{:S(2)}, u32[]{:S(2)}) collective-permute-start(bf16[2,3,64,384]{3,2,1,0:T(8,128)(2,1)S(1)} %copy-done.1), channel_id=1, source_target_pairs={{0,4},{1,5},{2,6},{3,7},{4,0},{5,1},{6,2},{7,3},{8,12},{9,13},{10,... | collective-permute-start | bytes 884744 | tf_op jit(solution)/shard_map/ppermute | solution.py:78
  34.8 2.1 %collective-permute-start.12 = (bf16[3,128,384]{2,1,0:T(8,128)(2,1)S(1)}, bf16[3,128,384]{2,1,0:T(8,128)(2,1)S(1)}, u32[]{:S(2)}, u32[]{:S(2)}) collective-permute-start(bf16[3,128,384]{2,1,0:T(8,128)(2,1)S(1)} %get-tuple-element.88), channel_id=1, source_target_pairs={{0,16},{1,17},{2,18},{3,19},{4,20},{5,21},{6,22},{7,23},{8,24},{9,... | collective-permute-start | bytes 884744 | tf_op jit(solution)/shard_map/ppermute | solution.py:78
  37.8 2.7 %collective-permute-done.15.refs_6_.refs_14_ = bf16[2,3,64,384]{3,2,1,0:T(8,128)(2,1)S(1)} collective-permute-done((bf16[2,3,64,384]{3,2,1,0:T(8,128)(2,1)S(1)}, bf16[2,3,64,384]{3,2,1,0:T(8,128)(2,1)S(1)}, u32[]{:S(2)}, u32[]{:S(2)}) %collective-permute-start.15) | collective-permute-done | bytes 294944 | tf_op jit(solution)/shard_map/ppermute | solution.py:78
  40.5 1.6 %collective-permute-start.17 = (bf16[3,64,384]{2,1,0:T(8,128)(2,1)S(1)}, bf16[3,64,384]{2,1,0:T(8,128)(2,1)S(1)}, u32[]{:S(2)}, u32[]{:S(2)}) collective-permute-start(bf16[3,64,384]{2,1,0:T(8,128)(2,1)S(1)} %slice_bitcast_fusion), channel_id=1, source_target_pairs={{0,4},{1,5},{2,6},{3,7},{4,0},{5,1},{6,2},{7,3},{8,12},{9,13},{10,... | collective-permute-start | bytes 442376 | tf_op jit(solution)/shard_map/ppermute | solution.py:78
  42.1 1.7 %collective-permute-start.16 = (bf16[3,64,384]{2,1,0:T(8,128)(2,1)S(1)}, bf16[3,64,384]{2,1,0:T(8,128)(2,1)S(1)}, u32[]{:S(2)}, u32[]{:S(2)}) collective-permute-start(bf16[3,64,384]{2,1,0:T(8,128)(2,1)S(1)} %slice_bitcast_fusion.1), channel_id=1, source_target_pairs={{0,8},{1,9},{2,10},{3,11},{4,12},{5,13},{6,14},{7,15},{8,0},{9,1},... | collective-permute-start | bytes 442376 | tf_op jit(solution)/shard_map/ppermute | solution.py:78
  43.9 7.8 %collective-permute-done.12.came_ref = bf16[3,128,384]{2,1,0:T(8,128)(2,1)S(1)} collective-permute-done((bf16[3,128,384]{2,1,0:T(8,128)(2,1)S(1)}, bf16[3,128,384]{2,1,0:T(8,128)(2,1)S(1)}, u32[]{:S(2)}, u32[]{:S(2)}) %collective-permute-start.12) | collective-permute-done | bytes 294944 | tf_op jit(solution)/shard_map/ppermute | solution.py:78
  58.1 13.5 %collective-permute-done.25.came_ref = bf16[3,128,384]{2,1,0:T(8,128)(2,1)S(1)} collective-permute-done((bf16[3,128,384]{2,1,0:T(8,128)(2,1)S(1)}, bf16[3,128,384]{2,1,0:T(8,128)(2,1)S(1)}, u32[]{:S(2)}, u32[]{:S(2)}) %collective-permute-start.25) | collective-permute-done | bytes 294944 | tf_op jit(solution)/shard_map/ppermute | solution.py:78
  72.4 2.6 %shard_map.118 = (bf16[2,32,1024]{2,1,0:T(8,128)(2,1)S(1)}, bf16[2,32,1024]{2,1,0:T(8,128)(2,1)S(1)}, bf16[2,32,1024]{2,1,0:T(8,128)(2,1)S(1)}, bf16[2,32,1024]{2,1,0:T(8,128)(2,1)S(1)}) custom-call(s32[4]{0:T(128)S(1)} %pad_add_fusion.at, bf16[3,128,384]{2,1,0:T(8,128)(2,1)S(1)} %shard_map.114.mine.refs_0_, ...), custom_call_target="tpu_custom_call" | custom-call | flops 603979776 | bytes 5832720 | tf_op jit(solution)/shard_map/pallas_call | solution.py:24
  77.8 2.0 %collective-permute-start.28 = (bf16[2,3,64,384]{3,2,1,0:T(8,128)(2,1)S(1)}, bf16[2,3,64,384]{3,2,1,0:T(8,128)(2,1)S(1)}, u32[]{:S(2)}, u32[]{:S(2)}) collective-permute-start(bf16[2,3,64,384]{3,2,1,0:T(8,128)(2,1)S(1)} %get-tuple-element.113), channel_id=1, source_target_pairs={{0,8},{1,9},{2,10},{3,11},{4,12},{5,13},{6,14},{7,15},{8,0},{9,1},... | collective-permute-start | bytes 884744 | tf_op jit(solution)/shard_map/ppermute | solution.py:78
  79.8 3.8 %collective-permute-start.31 = (bf16[2,32,1024]{2,1,0:T(8,128)(2,1)S(1)}, bf16[2,32,1024]{2,1,0:T(8,128)(2,1)S(1)}, u32[]{:S(2)}, u32[]{:S(2)}) collective-permute-start(bf16[2,32,1024]{2,1,0:T(8,128)(2,1)S(1)} %get-tuple-element.119), channel_id=1, source_target_pairs={{0,17},{1,16},{2,19},{3,18},{4,21},{5,20},{6,23},{7,22},{8,25},{9,... | collective-permute-start | bytes 393224 | tf_op jit(solution)/shard_map/ppermute | solution.py:78
  83.8 1.9 %collective-permute-done.27.from_first.refs_6_ = bf16[2,3,64,384]{3,2,1,0:T(8,128)(2,1)S(1)} collective-permute-done((bf16[2,3,64,384]{3,2,1,0:T(8,128)(2,1)S(1)}, bf16[2,3,64,384]{3,2,1,0:T(8,128)(2,1)S(1)}, u32[]{:S(2)}, u32[]{:S(2)}) %collective-permute-start.27) | collective-permute-done | bytes 294944 | tf_op jit(solution)/shard_map/ppermute | solution.py:78
  87.1 7.1 %collective-permute-done.28.from_second.refs_7_ = bf16[2,3,64,384]{3,2,1,0:T(8,128)(2,1)S(1)} collective-permute-done((bf16[2,3,64,384]{3,2,1,0:T(8,128)(2,1)S(1)}, bf16[2,3,64,384]{3,2,1,0:T(8,128)(2,1)S(1)}, u32[]{:S(2)}, u32[]{:S(2)}) %collective-permute-start.28) | collective-permute-done | bytes 294944 | tf_op jit(solution)/shard_map/ppermute | solution.py:78
  95.8 1.5 %collective-permute-start.29 = (bf16[2,32,1024]{2,1,0:T(8,128)(2,1)S(1)}, bf16[2,32,1024]{2,1,0:T(8,128)(2,1)S(1)}, u32[]{:S(2)}, u32[]{:S(2)}) collective-permute-start(bf16[2,32,1024]{2,1,0:T(8,128)(2,1)S(1)} %get-tuple-element.117), channel_id=1, source_target_pairs={{0,1},{1,0},{2,3},{3,2},{4,5},{5,4},{6,7},{7,6},{8,9},{9,8},{10,11... | collective-permute-start | bytes 393224 | tf_op jit(solution)/shard_map/ppermute | solution.py:78
  97.3 3.5 %collective-permute-done.29.refs_1_ = bf16[2,32,1024]{2,1,0:T(8,128)(2,1)S(1)} collective-permute-done((bf16[2,32,1024]{2,1,0:T(8,128)(2,1)S(1)}, bf16[2,32,1024]{2,1,0:T(8,128)(2,1)S(1)}, u32[]{:S(2)}, u32[]{:S(2)}) %collective-permute-start.29) | collective-permute-done | bytes 131104 | tf_op jit(solution)/shard_map/ppermute | solution.py:78
  100.7 2.5 %shard_map.121 = (bf16[192,2048]{1,0:T(8,128)(2,1)}, bf16[192,2048]{1,0:T(8,128)(2,1)}) custom-call(s32[4]{0:T(128)S(1)} %pad_add_fusion.at, f32[8,192]{1,0:T(8,128)S(1)} %get-tuple-element.75.p_ref, f32[8,192]{1,0:T(8,128)S(1)} %get-tuple-element.76.w_ref, bf16[2,32,1024]{2,1,0:T(8,128)(2,1)S(1)} %get-tuple-element.109.refs_0_, ...), custom_call_target="tpu_custom_call" | custom-call | bytes 2109456 | tf_op jit(solution)/shard_map/pallas_call | solution.py:24
  (83 shorter events, 24.0 us)
Async XLA Ops:
  3.1 12.6 %collective-permute-start.3 = (bf16[2,3,64,384]{3,2,1,0:T(8,128)(2,1)}, bf16[2,3,64,384]{3,2,1,0:T(8,128)(2,1)S(1)}, u32[]{:S(2)}, u32[]{:S(2)}) collective-permute-start(bf16[2,3,64,384]{3,2,1,0:T(8,128)(2,1)} %get-tuple-element.79.refs_4_.refs_2_), channel_id=1, source_target_pairs={{0,8},{1,9},{2,10},{3,11},{4,12},{5,13},{6,14},{7,15},{8,0},{9,1},... | collective-permute-start | bytes 884744 | tf_op jit(solution)/shard_map/ppermute | solution.py:78
  5.6 10.1 %collective-permute-start.2 = (bf16[2,3,64,384]{3,2,1,0:T(8,128)(2,1)}, bf16[2,3,64,384]{3,2,1,0:T(8,128)(2,1)S(1)}, u32[]{:S(2)}, u32[]{:S(2)}) collective-permute-start(bf16[2,3,64,384]{3,2,1,0:T(8,128)(2,1)} %get-tuple-element.79.refs_4_.refs_2_), channel_id=1, source_target_pairs={{0,4},{1,5},{2,6},{3,7},{4,0},{5,1},{6,2},{7,3},{8,12},{9,13},{10,... | collective-permute-start | bytes 884744 | tf_op jit(solution)/shard_map/ppermute | solution.py:78
  11.6 9.1 %collective-permute-start.4 = (bf16[2,32,1024]{2,1,0:T(8,128)(2,1)S(1)}, bf16[2,32,1024]{2,1,0:T(8,128)(2,1)S(1)}, u32[]{:S(2)}, u32[]{:S(2)}) collective-permute-start(bf16[2,32,1024]{2,1,0:T(8,128)(2,1)S(1)} %get-tuple-element.147), channel_id=1, source_target_pairs={{0,16},{1,17},{2,18},{3,19},{4,20},{5,21},{6,22},{7,23},{8,24},{9,... | collective-permute-start | bytes 393224 | tf_op jit(solution)/shard_map/ppermute | solution.py:78
  20.7 12.7 %collective-permute-start.9 = (bf16[2,3,64,384]{3,2,1,0:T(8,128)(2,1)S(1)}, bf16[2,3,64,384]{3,2,1,0:T(8,128)(2,1)S(1)}, u32[]{:S(2)}, u32[]{:S(2)}) collective-permute-start(bf16[2,3,64,384]{3,2,1,0:T(8,128)(2,1)S(1)} %collective-permute-done.3.refs_6_.refs_4_), channel_id=1, source_target_pairs={{0,2},{1,3},{2,0},{3,1},{4,6},{5,7},{6,4},{7,5},{8,10},{9,11},{10,... | collective-permute-start | bytes 884744 | tf_op jit(solution)/shard_map/ppermute | solution.py:78
  21.3 12.1 %collective-permute-start.8 = (bf16[2,3,64,384]{3,2,1,0:T(8,128)(2,1)S(1)}, bf16[2,3,64,384]{3,2,1,0:T(8,128)(2,1)S(1)}, u32[]{:S(2)}, u32[]{:S(2)}) collective-permute-start(bf16[2,3,64,384]{3,2,1,0:T(8,128)(2,1)S(1)} %collective-permute-done.2.refs_5_.refs_3_), channel_id=1, source_target_pairs={{0,2},{1,3},{2,0},{3,1},{4,6},{5,7},{6,4},{7,5},{8,10},{9,11},{10,... | collective-permute-start | bytes 884744 | tf_op jit(solution)/shard_map/ppermute | solution.py:78
  21.5 9.0 %collective-permute-start.6 = (bf16[3,64,384]{2,1,0:T(8,128)(2,1)S(1)}, bf16[3,64,384]{2,1,0:T(8,128)(2,1)S(1)}, u32[]{:S(2)}, u32[]{:S(2)}) collective-permute-start(bf16[3,64,384]{2,1,0:T(8,128)(2,1)S(1)} %slice_bitcast_fusion.3), channel_id=1, source_target_pairs={{0,8},{1,9},{2,10},{3,11},{4,12},{5,13},{6,14},{7,15},{8,0},{9,1},... | collective-permute-start | bytes 442376 | tf_op jit(solution)/shard_map/ppermute | solution.py:78
  30.5 10.0 %collective-permute-start.15 = (bf16[2,3,64,384]{3,2,1,0:T(8,128)(2,1)S(1)}, bf16[2,3,64,384]{3,2,1,0:T(8,128)(2,1)S(1)}, u32[]{:S(2)}, u32[]{:S(2)}) collective-permute-start(bf16[2,3,64,384]{3,2,1,0:T(8,128)(2,1)S(1)} %copy-done.1), channel_id=1, source_target_pairs={{0,8},{1,9},{2,10},{3,11},{4,12},{5,13},{6,14},{7,15},{8,0},{9,1},... | collective-permute-start | bytes 884744 | tf_op jit(solution)/shard_map/ppermute | solution.py:78
  31.9 10.2 %collective-permute-start.14 = (bf16[2,3,64,384]{3,2,1,0:T(8,128)(2,1)S(1)}, bf16[2,3,64,384]{3,2,1,0:T(8,128)(2,1)S(1)}, u32[]{:S(2)}, u32[]{:S(2)}) collective-permute-start(bf16[2,3,64,384]{3,2,1,0:T(8,128)(2,1)S(1)} %copy-done.1), channel_id=1, source_target_pairs={{0,4},{1,5},{2,6},{3,7},{4,0},{5,1},{6,2},{7,3},{8,12},{9,13},{10,... | collective-permute-start | bytes 884744 | tf_op jit(solution)/shard_map/ppermute | solution.py:78
  33.4 18.9 %collective-permute-start.18 = (bf16[2,3,64,384]{3,2,1,0:T(8,128)(2,1)S(1)}, bf16[2,3,64,384]{3,2,1,0:T(8,128)(2,1)S(1)}, u32[]{:S(2)}, u32[]{:S(2)}) collective-permute-start(bf16[2,3,64,384]{3,2,1,0:T(8,128)(2,1)S(1)} %copy-done.1), channel_id=1, source_target_pairs={{0,2},{1,3},{2,0},{3,1},{4,6},{5,7},{6,4},{7,5},{8,10},{9,11},{10,... | collective-permute-start | bytes 884744 | tf_op jit(solution)/shard_map/ppermute | solution.py:78
  34.8 16.8 %collective-permute-start.12 = (bf16[3,128,384]{2,1,0:T(8,128)(2,1)S(1)}, bf16[3,128,384]{2,1,0:T(8,128)(2,1)S(1)}, u32[]{:S(2)}, u32[]{:S(2)}) collective-permute-start(bf16[3,128,384]{2,1,0:T(8,128)(2,1)S(1)} %get-tuple-element.88), channel_id=1, source_target_pairs={{0,16},{1,17},{2,18},{3,19},{4,20},{5,21},{6,22},{7,23},{8,24},{9,... | collective-permute-start | bytes 884744 | tf_op jit(solution)/shard_map/ppermute | solution.py:78
  40.5 12.4 %collective-permute-start.17 = (bf16[3,64,384]{2,1,0:T(8,128)(2,1)S(1)}, bf16[3,64,384]{2,1,0:T(8,128)(2,1)S(1)}, u32[]{:S(2)}, u32[]{:S(2)}) collective-permute-start(bf16[3,64,384]{2,1,0:T(8,128)(2,1)S(1)} %slice_bitcast_fusion), channel_id=1, source_target_pairs={{0,4},{1,5},{2,6},{3,7},{4,0},{5,1},{6,2},{7,3},{8,12},{9,13},{10,... | collective-permute-start | bytes 442376 | tf_op jit(solution)/shard_map/ppermute | solution.py:78
  42.1 10.9 %collective-permute-start.16 = (bf16[3,64,384]{2,1,0:T(8,128)(2,1)S(1)}, bf16[3,64,384]{2,1,0:T(8,128)(2,1)S(1)}, u32[]{:S(2)}, u32[]{:S(2)}) collective-permute-start(bf16[3,64,384]{2,1,0:T(8,128)(2,1)S(1)} %slice_bitcast_fusion.1), channel_id=1, source_target_pairs={{0,8},{1,9},{2,10},{3,11},{4,12},{5,13},{6,14},{7,15},{8,0},{9,1},... | collective-permute-start | bytes 442376 | tf_op jit(solution)/shard_map/ppermute | solution.py:78
  43.9 10.7 %collective-permute-start.20 = (bf16[2,3,64,384]{3,2,1,0:T(8,128)(2,1)S(1)}, bf16[2,3,64,384]{3,2,1,0:T(8,128)(2,1)S(1)}, u32[]{:S(2)}, u32[]{:S(2)}) collective-permute-start(bf16[2,3,64,384]{3,2,1,0:T(8,128)(2,1)S(1)} %collective-permute-done.15.refs_6_.refs_14_), channel_id=1, source_target_pairs={{0,2},{1,3},{2,0},{3,1},{4,6},{5,7},{6,4},{7,5},{8,10},{9,11},{10,... | collective-permute-start | bytes 884744 | tf_op jit(solution)/shard_map/ppermute | solution.py:78
  55.9 15.7 %collective-permute-start.25 = (bf16[3,128,384]{2,1,0:T(8,128)(2,1)S(1)}, bf16[3,128,384]{2,1,0:T(8,128)(2,1)S(1)}, u32[]{:S(2)}, u32[]{:S(2)}) collective-permute-start(bf16[3,128,384]{2,1,0:T(8,128)(2,1)S(1)} %get-tuple-element.102), channel_id=1, source_target_pairs={{0,16},{1,17},{2,18},{3,19},{4,20},{5,21},{6,22},{7,23},{8,24},{9,... | collective-permute-start | bytes 884744 | tf_op jit(solution)/shard_map/ppermute | solution.py:78
  57.2 14.4 %collective-permute-start.24 = (bf16[2,3,64,384]{3,2,1,0:T(8,128)(2,1)S(1)}, bf16[2,3,64,384]{3,2,1,0:T(8,128)(2,1)S(1)}, u32[]{:S(2)}, u32[]{:S(2)}) collective-permute-start(bf16[2,3,64,384]{3,2,1,0:T(8,128)(2,1)S(1)} %get-tuple-element.100), channel_id=1, source_target_pairs={{0,4},{1,5},{2,6},{3,7},{4,0},{5,1},{6,2},{7,3},{8,12},{9,13},{10,... | collective-permute-start | bytes 884744 | tf_op jit(solution)/shard_map/ppermute | solution.py:78
  72.4 11.2 %collective-permute-start.32 = (bf16[2,3,64,384]{3,2,1,0:T(8,128)(2,1)S(1)}, bf16[2,3,64,384]{3,2,1,0:T(8,128)(2,1)S(1)}, u32[]{:S(2)}, u32[]{:S(2)}) collective-permute-start(bf16[2,3,64,384]{3,2,1,0:T(8,128)(2,1)S(1)} %get-tuple-element.124), channel_id=1, source_target_pairs={{0,8},{1,9},{2,10},{3,11},{4,12},{5,13},{6,14},{7,15},{8,0},{9,1},... | collective-permute-start | bytes 884744 | tf_op jit(solution)/shard_map/ppermute | solution.py:78
  76.3 9.4 %collective-permute-start.27 = (bf16[2,3,64,384]{3,2,1,0:T(8,128)(2,1)S(1)}, bf16[2,3,64,384]{3,2,1,0:T(8,128)(2,1)S(1)}, u32[]{:S(2)}, u32[]{:S(2)}) collective-permute-start(bf16[2,3,64,384]{3,2,1,0:T(8,128)(2,1)S(1)} %get-tuple-element.112), channel_id=1, source_target_pairs={{0,4},{1,5},{2,6},{3,7},{4,0},{5,1},{6,2},{7,3},{8,12},{9,13},{10,... | collective-permute-start | bytes 884744 | tf_op jit(solution)/shard_map/ppermute | solution.py:78
  77.8 16.4 %collective-permute-start.28 = (bf16[2,3,64,384]{3,2,1,0:T(8,128)(2,1)S(1)}, bf16[2,3,64,384]{3,2,1,0:T(8,128)(2,1)S(1)}, u32[]{:S(2)}, u32[]{:S(2)}) collective-permute-start(bf16[2,3,64,384]{3,2,1,0:T(8,128)(2,1)S(1)} %get-tuple-element.113), channel_id=1, source_target_pairs={{0,8},{1,9},{2,10},{3,11},{4,12},{5,13},{6,14},{7,15},{8,0},{9,1},... | collective-permute-start | bytes 884744 | tf_op jit(solution)/shard_map/ppermute | solution.py:78
  79.8 14.6 %collective-permute-start.30 = (bf16[2,32,1024]{2,1,0:T(8,128)(2,1)S(1)}, bf16[2,32,1024]{2,1,0:T(8,128)(2,1)S(1)}, u32[]{:S(2)}, u32[]{:S(2)}) collective-permute-start(bf16[2,32,1024]{2,1,0:T(8,128)(2,1)S(1)} %get-tuple-element.118), channel_id=1, source_target_pairs={{0,16},{1,17},{2,18},{3,19},{4,20},{5,21},{6,22},{7,23},{8,24},{9,... | collective-permute-start | bytes 393224 | tf_op jit(solution)/shard_map/ppermute | solution.py:78
  79.8 16.0 %collective-permute-start.31 = (bf16[2,32,1024]{2,1,0:T(8,128)(2,1)S(1)}, bf16[2,32,1024]{2,1,0:T(8,128)(2,1)S(1)}, u32[]{:S(2)}, u32[]{:S(2)}) collective-permute-start(bf16[2,32,1024]{2,1,0:T(8,128)(2,1)S(1)} %get-tuple-element.119), channel_id=1, source_target_pairs={{0,17},{1,16},{2,19},{3,18},{4,21},{5,20},{6,23},{7,22},{8,25},{9,... | collective-permute-start | bytes 393224 | tf_op jit(solution)/shard_map/ppermute | solution.py:78
  83.7 19.6 %collective-permute-start.33 = (bf16[3,64,384]{2,1,0:T(8,128)(2,1)S(1)}, bf16[3,64,384]{2,1,0:T(8,128)(2,1)S(1)}, u32[]{:S(2)}, u32[]{:S(2)}) collective-permute-start(bf16[3,64,384]{2,1,0:T(8,128)(2,1)S(1)} %get-tuple-element.126), channel_id=1, source_target_pairs={{0,8},{1,9},{2,10},{3,11},{4,12},{5,13},{6,14},{7,15},{8,0},{9,1},... | collective-permute-start | bytes 442376 | tf_op jit(solution)/shard_map/ppermute | solution.py:78
  85.7 17.5 %collective-permute-start.34 = (bf16[3,64,384]{2,1,0:T(8,128)(2,1)S(1)}, bf16[3,64,384]{2,1,0:T(8,128)(2,1)S(1)}, u32[]{:S(2)}, u32[]{:S(2)}) collective-permute-start(bf16[3,64,384]{2,1,0:T(8,128)(2,1)S(1)} %get-tuple-element.127), channel_id=1, source_target_pairs={{0,4},{1,5},{2,6},{3,7},{4,0},{5,1},{6,2},{7,3},{8,12},{9,13},{10,... | collective-permute-start | bytes 442376 | tf_op jit(solution)/shard_map/ppermute | solution.py:78
  94.2 9.0 %collective-permute-start.35 = (bf16[3,64,384]{2,1,0:T(8,128)(2,1)S(1)}, bf16[3,64,384]{2,1,0:T(8,128)(2,1)S(1)}, u32[]{:S(2)}, u32[]{:S(2)}) collective-permute-start(bf16[3,64,384]{2,1,0:T(8,128)(2,1)S(1)} %get-tuple-element.129), channel_id=1, source_target_pairs={{0,8},{1,9},{2,10},{3,11},{4,12},{5,13},{6,14},{7,15},{8,0},{9,1},... | collective-permute-start | bytes 442376 | tf_op jit(solution)/shard_map/ppermute | solution.py:78
  94.3 8.9 %collective-permute-start.36 = (bf16[3,64,384]{2,1,0:T(8,128)(2,1)S(1)}, bf16[3,64,384]{2,1,0:T(8,128)(2,1)S(1)}, u32[]{:S(2)}, u32[]{:S(2)}) collective-permute-start(bf16[3,64,384]{2,1,0:T(8,128)(2,1)S(1)} %get-tuple-element.130), channel_id=1, source_target_pairs={{0,4},{1,5},{2,6},{3,7},{4,0},{5,1},{6,2},{7,3},{8,12},{9,13},{10,... | collective-permute-start | bytes 442376 | tf_op jit(solution)/shard_map/ppermute | solution.py:78
  (19 other events, 83.9 us)

commit v4 on v3

--- a/solution.py
+++ b/solution.py
@@ -212,7 +212,9 @@
     )
     across = send(leave, core=1)
 
-    cames[0], across = lax.optimization_barrier((cames[0], across))
+    early = parts[-1][reach:-2]
+    cames[0], across, early = lax.optimization_barrier((cames[0], across, early))
+    parts[-1][reach:-2] = early
     for i in range(1, PARTS):
         cames.append(send(gives[i], half=1))
 
@@ -334,7 +336,7 @@
     for i, (h, s) in enumerate(spots):
         if h > 0:
             home[h, s] = send(back[i], half=h, shift=-s)
-    joined, near_back = lax.optimization_barrier((joined, tuple(back[1:experts])))
+    hop[0], near_back = lax.optimization_barrier((hop[0], tuple(back[1:experts])))
     for s in range(1, experts):
         home[0, s] = send(near_back[s - 1], shift=-s)
     home = [home[spot] for spot in spots]
@@ -342,23 +344,27 @@
 
     def collect(at, p_ref, w_ref, *refs):
         ins, (out, d_in) = refs[: len(spots)], refs[len(spots) :]
-        picks = [selector(p_ref[s : s + 1]).astype(bf16) for s in range(experts)]
-        columns = jnp.transpose(w_ref[...])
+        picks, coarse, fine = [], [], []
+        for s in range(experts):
+            pick = selector(p_ref[s : s + 1])
+            heavy = pick * w_ref[s : s + 1]
+            picks.append(pick.astype(bf16))
+            coarse.append(heavy.astype(bf16))
+            fine.append((heavy - coarse[s].astype(f32)).astype(bf16))
+        picks = jnp.concatenate(picks, axis=0)
+        scaled = jnp.concatenate(coarse + fine, axis=0)
         for h in range(HALVES):
             side = jnp.bitwise_xor(at[0], h)
             cols = pl.ds(pl.multiple_of(side * span, span), span)
-            total_out = jnp.zeros((count, span), f32)
-            total_in = jnp.zeros((count, span), f32)
-            for s in range(experts):
-                ref = ins[h * experts + s]
-                total_out += columns[:, s : s + 1] * lax.dot_general(
-                    picks[s], ref[0], CONTRACT_FIRST, preferred_element_type=f32
-                )
-                total_in += lax.dot_general(
-                    picks[s], ref[1], CONTRACT_FIRST, preferred_element_type=f32
-                )
-            out[:, cols] = total_out.astype(bf16)
-            d_in[:, cols] = total_in.astype(bf16)
+            part = ins[h * experts : (h + 1) * experts]
+            rows_out = jnp.concatenate([ref[0] for ref in part] * 2, axis=0)
+            rows_in = jnp.concatenate([ref[1] for ref in part], axis=0)
+            out[:, cols] = lax.dot_general(
+                scaled, rows_out, CONTRACT_FIRST, preferred_element_type=f32
+            ).astype(bf16)
+            d_in[:, cols] = lax.dot_general(
+                picks, rows_in, CONTRACT_FIRST, preferred_element_type=f32
+            ).astype(bf16)
 
     layer_out, d_tokens = call(
         collect, [shape(count, width)] * 2, [here, places, weights, *home]

time: 105 us -> 103 us (0.981)
  starting transfers between devices: 33.9 us -> 28.2 us
  waiting for transfers between devices: 49.7 us -> 53.6 us
    ppermute x37, starting transfers between devices: 33.9 us -> 28.2 us  [send(): return lax.ppermute(value, ('dp', 'expert'), perm)]
    ppermute x37, waiting for transfers between devices: 49.7 us -> 53.6 us  [send(): return lax.ppermute(value, ('dp', 'expert'), perm)]
  transfers between devices with their start and end apart: 37 -> 37, of which waited for: 13 -> 15; matrix products, arithmetic and copies ran while one was open for 0% -> 0% of each run, Pallas kernels for 12% -> 12%
where the time goes in v4:
time: 103 us; the launch traced here: 102 us
  waiting for transfers between devices  53.6 us (52%)
  starting transfers between devices  28.2 us (27%)
  Pallas kernels  16.5 us (16%)
  local copies, waits for them, and re-layouts  3.02 us (3%)
    ppermute x37, waiting for transfers between devices, send(): return lax.ppermute(value, ('dp', 'expert'), perm)  53.6 us
    ppermute x37, starting transfers between devices, send(): return lax.ppermute(value, ('dp', 'expert'), perm)  28.2 us
    pallas_call x13, Pallas kernels, call(): pl.pallas_call(kernel, out_shape=out_shape, in_specs=[pl.BlockSpec(memory...  14.5 us
    unnamed x12, local copies, waits for them, and re-layouts  2.91 us
  transfers between devices with their start and end apart: 37, of which 15 were waited for; matrix products, arithmetic and copies ran while one was open for 0% of the time, Pallas kernels for 12%

profile of v4, /device:TPU:0, one launch (start us, length us, event | category | flops | bytes accessed | tf_op | source)
XLA Modules:
  0.0 102.3 jit_solution(6952493446686366541)
XLA Ops:
  0.6 2.0 %shard_map.111 = (bf16[2,3,64,384]{3,2,1,0:T(8,128)(2,1)}, bf16[2,3,64,384]{3,2,1,0:T(8,128)(2,1)}) custom-call(bf16[1,128,768]{2,1,0:T(8,128)(2,1)} %g_ref.1, bf16[1,128,768]{2,1,0:T(8,128)(2,1)} %u_ref.1, bf16[1,128,768]{2,1,0:T(8,128)(2,1)} %w_ref.1), custom_call_target="tpu_custom_call" | custom-call | tf_op jit(solution)/shard_map/pallas_call | solution.py:96
  3.1 2.6 %collective-permute-start.3 = (bf16[2,3,64,384]{3,2,1,0:T(8,128)(2,1)}, bf16[2,3,64,384]{3,2,1,0:T(8,128)(2,1)S(1)}, u32[]{:S(2)}, u32[]{:S(2)}) collective-permute-start(bf16[2,3,64,384]{3,2,1,0:T(8,128)(2,1)} %get-tuple-element.81.refs_4_.refs_2_), channel_id=1, source_target_pairs={{0,8},{1,9},{2,10},{3,11},{4,12},{5,13},{6,14},{7,15},{8,0},{9,1},... | collective-permute-start | bytes 884744 | tf_op jit(solution)/shard_map/ppermute | solution.py:78
  5.6 1.5 %collective-permute-start.2 = (bf16[2,3,64,384]{3,2,1,0:T(8,128)(2,1)}, bf16[2,3,64,384]{3,2,1,0:T(8,128)(2,1)S(1)}, u32[]{:S(2)}, u32[]{:S(2)}) collective-permute-start(bf16[2,3,64,384]{3,2,1,0:T(8,128)(2,1)} %get-tuple-element.81.refs_4_.refs_2_), channel_id=1, source_target_pairs={{0,4},{1,5},{2,6},{3,7},{4,0},{5,1},{6,2},{7,3},{8,12},{9,13},{10,... | collective-permute-start | bytes 884744 | tf_op jit(solution)/shard_map/ppermute | solution.py:78
  10.1 1.4 %shard_map.110 = (bf16[2,2,32,1024]{3,2,1,0:T(8,128)(2,1)S(1)}, bf16[2,2,32,1024]{3,2,1,0:T(8,128)(2,1)S(1)}, f32[8,192]{1,0:T(8,128)S(1)}, f32[8,192]{1,0:T(8,128)S(1)}) custom-call(s32[4]{0:T(128)S(1)} %pad_add_fusion.at, s32[6,192]{1,0:T(8,128)S(1)} %bitcast.22, f32[6,192]{1,0:T(8,128)S(1)} %bitcast.23, bf16[192,2048]{1,0:T(8,128)(2,1)S(1)} %copy-done.2, ...), custom_call_target="tpu_custom_call" | custom-call | bytes 2118672 | tf_op jit(solution)/shard_map/pallas_call | solution.py:24
  11.6 2.7 %collective-permute-start.4 = (bf16[2,32,1024]{2,1,0:T(8,128)(2,1)S(1)}, bf16[2,32,1024]{2,1,0:T(8,128)(2,1)S(1)}, u32[]{:S(2)}, u32[]{:S(2)}) collective-permute-start(bf16[2,32,1024]{2,1,0:T(8,128)(2,1)S(1)} %get-tuple-element.151), channel_id=1, source_target_pairs={{0,16},{1,17},{2,18},{3,19},{4,20},{5,21},{6,22},{7,23},{8,24},{9,... | collective-permute-start | bytes 393224 | tf_op jit(solution)/shard_map/ppermute | solution.py:78
  14.2 1.5 %collective-permute-start.1 = (bf16[2,2,32,1024]{3,2,1,0:T(8,128)(2,1)S(1)}, bf16[2,2,32,1024]{3,2,1,0:T(8,128)(2,1)S(1)}, u32[]{:S(2)}, u32[]{:S(2)}) collective-permute-start(bf16[2,2,32,1024]{3,2,1,0:T(8,128)(2,1)S(1)} %get-tuple-element.83), channel_id=1, source_target_pairs={{0,1},{1,0},{2,3},{3,2},{4,5},{5,4},{6,7},{7,6},{8,9},{9,8},{10,11... | collective-permute-start | bytes 786440 | tf_op jit(solution)/shard_map/ppermute | solution.py:78
  15.7 5.0 %collective-permute-done.4.refs_2_ = bf16[2,32,1024]{2,1,0:T(8,128)(2,1)S(1)} collective-permute-done((bf16[2,32,1024]{2,1,0:T(8,128)(2,1)S(1)}, bf16[2,32,1024]{2,1,0:T(8,128)(2,1)S(1)}, u32[]{:S(2)}, u32[]{:S(2)}) %collective-permute-start.4) | collective-permute-done | bytes 131104 | tf_op jit(solution)/shard_map/ppermute | solution.py:78
  22.1 2.4 %collective-permute-start.5 = (bf16[2,32,1024]{2,1,0:T(8,128)(2,1)S(1)}, bf16[2,32,1024]{2,1,0:T(8,128)(2,1)S(1)}, u32[]{:S(2)}, u32[]{:S(2)}) collective-permute-start(bf16[2,32,1024]{2,1,0:T(8,128)(2,1)S(1)} %get-tuple-element.149), channel_id=1, source_target_pairs={{0,16},{1,17},{2,18},{3,19},{4,20},{5,21},{6,22},{7,23},{8,24},{9,... | collective-permute-start | bytes 393224 | tf_op jit(solution)/shard_map/ppermute | solution.py:78
  24.5 1.4 %collective-permute-done.7.refs_8_.refs_6_ = bf16[3,64,384]{2,1,0:T(8,128)(2,1)S(1)} collective-permute-done((bf16[3,64,384]{2,1,0:T(8,128)(2,1)S(1)}, bf16[3,64,384]{2,1,0:T(8,128)(2,1)S(1)}, u32[]{:S(2)}, u32[]{:S(2)}) %collective-permute-start.7) | collective-permute-done | bytes 147488 | tf_op jit(solution)/shard_map/ppermute | solution.py:78
  26.5 2.0 %collective-permute-done.6.refs_7_.refs_5_ = bf16[3,64,384]{2,1,0:T(8,128)(2,1)S(1)} collective-permute-done((bf16[3,64,384]{2,1,0:T(8,128)(2,1)S(1)}, bf16[3,64,384]{2,1,0:T(8,128)(2,1)S(1)}, u32[]{:S(2)}, u32[]{:S(2)}) %collective-permute-start.6) | collective-permute-done | bytes 147488 | tf_op jit(solution)/shard_map/ppermute | solution.py:78
  28.5 1.6 %collective-permute-done.5.refs_3_ = bf16[2,32,1024]{2,1,0:T(8,128)(2,1)S(1)} collective-permute-done((bf16[2,32,1024]{2,1,0:T(8,128)(2,1)S(1)}, bf16[2,32,1024]{2,1,0:T(8,128)(2,1)S(1)}, u32[]{:S(2)}, u32[]{:S(2)}) %collective-permute-start.5) | collective-permute-done | bytes 131104 | tf_op jit(solution)/shard_map/ppermute | solution.py:78
  31.4 1.4 %collective-permute-done.10.refs_12_.refs_10_ = bf16[3,64,384]{2,1,0:T(8,128)(2,1)S(1)} collective-permute-done((bf16[3,64,384]{2,1,0:T(8,128)(2,1)S(1)}, bf16[3,64,384]{2,1,0:T(8,128)(2,1)S(1)}, u32[]{:S(2)}, u32[]{:S(2)}) %collective-permute-start.10) | collective-permute-done | bytes 147488 | tf_op jit(solution)/shard_map/ppermute | solution.py:78
  32.9 1.3 %shard_map.112 = (f32[3,128,384]{2,1,0:T(8,128)S(1)}, bf16[3,128,384]{2,1,0:T(8,128)(2,1)S(1)}) custom-call(s32[4]{0:T(128)S(1)} %pad_add_fusion.at, bf16[2,32,1024]{2,1,0:T(8,128)(2,1)S(1)} %get-tuple-element.91.refs_0_, bf16[2,32,1024]{2,1,0:T(8,128)(2,1)S(1)} %get-tuple-element.92.refs_1_, bf16[2,32,1024]{2,1,0:T(8,128)(2,1)S(1)} %collective-permute-done.4.refs_2_, ...), custom_call_target="tpu_custom_call" | custom-call | flops 301989888 | bytes 3768336 | tf_op jit(solution)/shard_map/pallas_call | solution.py:24
  36.9 1.4 %collective-permute-start.20 = (bf16[3,64,384]{2,1,0:T(8,128)(2,1)S(1)}, bf16[3,64,384]{2,1,0:T(8,128)(2,1)S(1)}, u32[]{:S(2)}, u32[]{:S(2)}) collective-permute-start(bf16[3,64,384]{2,1,0:T(8,128)(2,1)S(1)} %slice_bitcast_fusion), channel_id=1, source_target_pairs={{0,4},{1,5},{2,6},{3,7},{4,0},{5,1},{6,2},{7,3},{8,12},{9,13},{10,... | collective-permute-start | bytes 442376 | tf_op jit(solution)/shard_map/ppermute | solution.py:78
  39.5 11.4 %collective-permute-done.12.came_ref = bf16[3,128,384]{2,1,0:T(8,128)(2,1)S(1)} collective-permute-done((bf16[3,128,384]{2,1,0:T(8,128)(2,1)S(1)}, bf16[3,128,384]{2,1,0:T(8,128)(2,1)S(1)}, u32[]{:S(2)}, u32[]{:S(2)}) %collective-permute-start.12) | collective-permute-done | bytes 294944 | tf_op jit(solution)/shard_map/ppermute | solution.py:78
  57.0 13.7 %collective-permute-done.25.came_ref = bf16[3,128,384]{2,1,0:T(8,128)(2,1)S(1)} collective-permute-done((bf16[3,128,384]{2,1,0:T(8,128)(2,1)S(1)}, bf16[3,128,384]{2,1,0:T(8,128)(2,1)S(1)}, u32[]{:S(2)}, u32[]{:S(2)}) %collective-permute-start.25) | collective-permute-done | bytes 294944 | tf_op jit(solution)/shard_map/ppermute | solution.py:78
  71.5 2.6 %shard_map.118 = (bf16[2,32,1024]{2,1,0:T(8,128)(2,1)S(1)}, bf16[2,32,1024]{2,1,0:T(8,128)(2,1)S(1)}, bf16[2,32,1024]{2,1,0:T(8,128)(2,1)S(1)}, bf16[2,32,1024]{2,1,0:T(8,128)(2,1)S(1)}) custom-call(s32[4]{0:T(128)S(1)} %pad_add_fusion.at, bf16[3,128,384]{2,1,0:T(8,128)(2,1)S(1)} %shard_map.114.mine.refs_0_, ...), custom_call_target="tpu_custom_call" | custom-call | flops 603979776 | bytes 5832720 | tf_op jit(solution)/shard_map/pallas_call | solution.py:24
  76.0 2.0 %collective-permute-start.34 = (bf16[2,3,64,384]{3,2,1,0:T(8,128)(2,1)S(1)}, bf16[2,3,64,384]{3,2,1,0:T(8,128)(2,1)S(1)}, u32[]{:S(2)}, u32[]{:S(2)}) collective-permute-start(bf16[2,3,64,384]{3,2,1,0:T(8,128)(2,1)S(1)} %get-tuple-element.131), channel_id=1, source_target_pairs={{0,8},{1,9},{2,10},{3,11},{4,12},{5,13},{6,14},{7,15},{8,0},{9,1},... | collective-permute-start | bytes 884744 | tf_op jit(solution)/shard_map/ppermute | solution.py:78
  78.4 3.4 %collective-permute-start.30 = (bf16[2,32,1024]{2,1,0:T(8,128)(2,1)S(1)}, bf16[2,32,1024]{2,1,0:T(8,128)(2,1)S(1)}, u32[]{:S(2)}, u32[]{:S(2)}) collective-permute-start(bf16[2,32,1024]{2,1,0:T(8,128)(2,1)S(1)} %get-tuple-element.120), channel_id=1, source_target_pairs={{0,17},{1,16},{2,19},{3,18},{4,21},{5,20},{6,23},{7,22},{8,25},{9,... | collective-permute-start | bytes 393224 | tf_op jit(solution)/shard_map/ppermute | solution.py:78
  81.9 5.0 %collective-permute-done.31.from_second.refs_2_ = bf16[2,3,64,384]{3,2,1,0:T(8,128)(2,1)S(1)} collective-permute-done((bf16[2,3,64,384]{3,2,1,0:T(8,128)(2,1)S(1)}, bf16[2,3,64,384]{3,2,1,0:T(8,128)(2,1)S(1)}, u32[]{:S(2)}, u32[]{:S(2)}) %collective-permute-start.31) | collective-permute-done | bytes 294944 | tf_op jit(solution)/shard_map/ppermute | solution.py:78
  87.1 6.1 %collective-permute-done.34.from_second.refs_7_ = bf16[2,3,64,384]{3,2,1,0:T(8,128)(2,1)S(1)} collective-permute-done((bf16[2,3,64,384]{3,2,1,0:T(8,128)(2,1)S(1)}, bf16[2,3,64,384]{3,2,1,0:T(8,128)(2,1)S(1)}, u32[]{:S(2)}, u32[]{:S(2)}) %collective-permute-start.34) | collective-permute-done | bytes 294944 | tf_op jit(solution)/shard_map/ppermute | solution.py:78
  94.0 1.5 %collective-permute-start.28 = (bf16[2,32,1024]{2,1,0:T(8,128)(2,1)S(1)}, bf16[2,32,1024]{2,1,0:T(8,128)(2,1)S(1)}, u32[]{:S(2)}, u32[]{:S(2)}) collective-permute-start(bf16[2,32,1024]{2,1,0:T(8,128)(2,1)S(1)} %get-tuple-element.118), channel_id=1, source_target_pairs={{0,1},{1,0},{2,3},{3,2},{4,5},{5,4},{6,7},{7,6},{8,9},{9,8},{10,11... | collective-permute-start | bytes 393224 | tf_op jit(solution)/shard_map/ppermute | solution.py:78
  95.5 3.5 %collective-permute-done.28.refs_1_ = bf16[2,32,1024]{2,1,0:T(8,128)(2,1)S(1)} collective-permute-done((bf16[2,32,1024]{2,1,0:T(8,128)(2,1)S(1)}, bf16[2,32,1024]{2,1,0:T(8,128)(2,1)S(1)}, u32[]{:S(2)}, u32[]{:S(2)}) %collective-permute-start.28) | collective-permute-done | bytes 131104 | tf_op jit(solution)/shard_map/ppermute | solution.py:78
  99.0 2.2 %shard_map.120 = (bf16[192,2048]{1,0:T(8,128)(2,1)}, bf16[192,2048]{1,0:T(8,128)(2,1)}) custom-call(s32[4]{0:T(128)S(1)} %pad_add_fusion.at, f32[8,192]{1,0:T(8,128)S(1)} %get-tuple-element.77.p_ref, f32[8,192]{1,0:T(8,128)S(1)} %get-tuple-element.78.w_ref, bf16[2,32,1024]{2,1,0:T(8,128)(2,1)S(1)} %get-tuple-element.114.refs_0_, ...), custom_call_target="tpu_custom_call" | custom-call | bytes 2109456 | tf_op jit(solution)/shard_map/pallas_call | solution.py:24
  (83 shorter events, 21.9 us)
Async XLA Ops:
  2.6 8.9 %collective-permute-start = (bf16[2,3,64,384]{3,2,1,0:T(8,128)(2,1)}, bf16[2,3,64,384]{3,2,1,0:T(8,128)(2,1)S(1)}, u32[]{:S(2)}, u32[]{:S(2)}) collective-permute-start(bf16[2,3,64,384]{3,2,1,0:T(8,128)(2,1)} %get-tuple-element.81.refs_4_.refs_2_), channel_id=1, source_target_pairs={{0,2},{1,3},{2,0},{3,1},{4,6},{5,7},{6,4},{7,5},{8,10},{9,11},{10,... | collective-permute-start | bytes 884744 | tf_op jit(solution)/shard_map/ppermute | solution.py:78
  3.1 12.6 %collective-permute-start.3 = (bf16[2,3,64,384]{3,2,1,0:T(8,128)(2,1)}, bf16[2,3,64,384]{3,2,1,0:T(8,128)(2,1)S(1)}, u32[]{:S(2)}, u32[]{:S(2)}) collective-permute-start(bf16[2,3,64,384]{3,2,1,0:T(8,128)(2,1)} %get-tuple-element.81.refs_4_.refs_2_), channel_id=1, source_target_pairs={{0,8},{1,9},{2,10},{3,11},{4,12},{5,13},{6,14},{7,15},{8,0},{9,1},... | collective-permute-start | bytes 884744 | tf_op jit(solution)/shard_map/ppermute | solution.py:78
  5.6 10.1 %collective-permute-start.2 = (bf16[2,3,64,384]{3,2,1,0:T(8,128)(2,1)}, bf16[2,3,64,384]{3,2,1,0:T(8,128)(2,1)S(1)}, u32[]{:S(2)}, u32[]{:S(2)}) collective-permute-start(bf16[2,3,64,384]{3,2,1,0:T(8,128)(2,1)} %get-tuple-element.81.refs_4_.refs_2_), channel_id=1, source_target_pairs={{0,4},{1,5},{2,6},{3,7},{4,0},{5,1},{6,2},{7,3},{8,12},{9,13},{10,... | collective-permute-start | bytes 884744 | tf_op jit(solution)/shard_map/ppermute | solution.py:78
  11.6 9.1 %collective-permute-start.4 = (bf16[2,32,1024]{2,1,0:T(8,128)(2,1)S(1)}, bf16[2,32,1024]{2,1,0:T(8,128)(2,1)S(1)}, u32[]{:S(2)}, u32[]{:S(2)}) collective-permute-start(bf16[2,32,1024]{2,1,0:T(8,128)(2,1)S(1)} %get-tuple-element.151), channel_id=1, source_target_pairs={{0,16},{1,17},{2,18},{3,19},{4,20},{5,21},{6,22},{7,23},{8,24},{9,... | collective-permute-start | bytes 393224 | tf_op jit(solution)/shard_map/ppermute | solution.py:78
  14.2 7.9 %collective-permute-start.1 = (bf16[2,2,32,1024]{3,2,1,0:T(8,128)(2,1)S(1)}, bf16[2,2,32,1024]{3,2,1,0:T(8,128)(2,1)S(1)}, u32[]{:S(2)}, u32[]{:S(2)}) collective-permute-start(bf16[2,2,32,1024]{3,2,1,0:T(8,128)(2,1)S(1)} %get-tuple-element.83), channel_id=1, source_target_pairs={{0,1},{1,0},{2,3},{3,2},{4,5},{5,4},{6,7},{7,6},{8,9},{9,8},{10,11... | collective-permute-start | bytes 786440 | tf_op jit(solution)/shard_map/ppermute | solution.py:78
  21.3 7.2 %collective-permute-start.6 = (bf16[3,64,384]{2,1,0:T(8,128)(2,1)S(1)}, bf16[3,64,384]{2,1,0:T(8,128)(2,1)S(1)}, u32[]{:S(2)}, u32[]{:S(2)}) collective-permute-start(bf16[3,64,384]{2,1,0:T(8,128)(2,1)S(1)} %slice_bitcast_fusion.3), channel_id=1, source_target_pairs={{0,8},{1,9},{2,10},{3,11},{4,12},{5,13},{6,14},{7,15},{8,0},{9,1},... | collective-permute-start | bytes 442376 | tf_op jit(solution)/shard_map/ppermute | solution.py:78
  22.1 8.1 %collective-permute-start.5 = (bf16[2,32,1024]{2,1,0:T(8,128)(2,1)S(1)}, bf16[2,32,1024]{2,1,0:T(8,128)(2,1)S(1)}, u32[]{:S(2)}, u32[]{:S(2)}) collective-permute-start(bf16[2,32,1024]{2,1,0:T(8,128)(2,1)S(1)} %get-tuple-element.149), channel_id=1, source_target_pairs={{0,16},{1,17},{2,18},{3,19},{4,20},{5,21},{6,22},{7,23},{8,24},{9,... | collective-permute-start | bytes 393224 | tf_op jit(solution)/shard_map/ppermute | solution.py:78
  28.5 7.8 %collective-permute-start.17 = (bf16[2,3,64,384]{3,2,1,0:T(8,128)(2,1)S(1)}, bf16[2,3,64,384]{3,2,1,0:T(8,128)(2,1)S(1)}, u32[]{:S(2)}, u32[]{:S(2)}) collective-permute-start(bf16[2,3,64,384]{3,2,1,0:T(8,128)(2,1)S(1)} %copy-done.1), channel_id=1, source_target_pairs={{0,8},{1,9},{2,10},{3,11},{4,12},{5,13},{6,14},{7,15},{8,0},{9,1},... | collective-permute-start | bytes 884744 | tf_op jit(solution)/shard_map/ppermute | solution.py:78
  34.3 16.6 %collective-permute-start.12 = (bf16[3,128,384]{2,1,0:T(8,128)(2,1)S(1)}, bf16[3,128,384]{2,1,0:T(8,128)(2,1)S(1)}, u32[]{:S(2)}, u32[]{:S(2)}) collective-permute-start(bf16[3,128,384]{2,1,0:T(8,128)(2,1)S(1)} %get-tuple-element.90), channel_id=1, source_target_pairs={{0,16},{1,17},{2,18},{3,19},{4,20},{5,21},{6,22},{7,23},{8,24},{9,... | collective-permute-start | bytes 884744 | tf_op jit(solution)/shard_map/ppermute | solution.py:78
  36.3 14.5 %collective-permute-start.18 = (bf16[2,3,64,384]{3,2,1,0:T(8,128)(2,1)S(1)}, bf16[2,3,64,384]{3,2,1,0:T(8,128)(2,1)S(1)}, u32[]{:S(2)}, u32[]{:S(2)}) collective-permute-start(bf16[2,3,64,384]{3,2,1,0:T(8,128)(2,1)S(1)} %collective-permute-done.17.refs_6_.refs_14_), channel_id=1, source_target_pairs={{0,2},{1,3},{2,0},{3,1},{4,6},{5,7},{6,4},{7,5},{8,10},{9,11},{10,... | collective-permute-start | bytes 884744 | tf_op jit(solution)/shard_map/ppermute | solution.py:78
  36.9 14.0 %collective-permute-start.16 = (bf16[2,3,64,384]{3,2,1,0:T(8,128)(2,1)S(1)}, bf16[2,3,64,384]{3,2,1,0:T(8,128)(2,1)S(1)}, u32[]{:S(2)}, u32[]{:S(2)}) collective-permute-start(bf16[2,3,64,384]{3,2,1,0:T(8,128)(2,1)S(1)} %collective-permute-done.15.refs_5_.refs_13_), channel_id=1, source_target_pairs={{0,2},{1,3},{2,0},{3,1},{4,6},{5,7},{6,4},{7,5},{8,10},{9,11},{10,... | collective-permute-start | bytes 884744 | tf_op jit(solution)/shard_map/ppermute | solution.py:78
  36.9 14.7 %collective-permute-start.20 = (bf16[3,64,384]{2,1,0:T(8,128)(2,1)S(1)}, bf16[3,64,384]{2,1,0:T(8,128)(2,1)S(1)}, u32[]{:S(2)}, u32[]{:S(2)}) collective-permute-start(bf16[3,64,384]{2,1,0:T(8,128)(2,1)S(1)} %slice_bitcast_fusion), channel_id=1, source_target_pairs={{0,4},{1,5},{2,6},{3,7},{4,0},{5,1},{6,2},{7,3},{8,12},{9,13},{10,... | collective-permute-start | bytes 442376 | tf_op jit(solution)/shard_map/ppermute | solution.py:78
  38.3 13.8 %collective-permute-start.19 = (bf16[3,64,384]{2,1,0:T(8,128)(2,1)S(1)}, bf16[3,64,384]{2,1,0:T(8,128)(2,1)S(1)}, u32[]{:S(2)}, u32[]{:S(2)}) collective-permute-start(bf16[3,64,384]{2,1,0:T(8,128)(2,1)S(1)} %slice_bitcast_fusion.1), channel_id=1, source_target_pairs={{0,8},{1,9},{2,10},{3,11},{4,12},{5,13},{6,14},{7,15},{8,0},{9,1},... | collective-permute-start | bytes 442376 | tf_op jit(solution)/shard_map/ppermute | solution.py:78
  54.9 15.7 %collective-permute-start.25 = (bf16[3,128,384]{2,1,0:T(8,128)(2,1)S(1)}, bf16[3,128,384]{2,1,0:T(8,128)(2,1)S(1)}, u32[]{:S(2)}, u32[]{:S(2)}) collective-permute-start(bf16[3,128,384]{2,1,0:T(8,128)(2,1)S(1)} %get-tuple-element.104), channel_id=1, source_target_pairs={{0,16},{1,17},{2,18},{3,19},{4,20},{5,21},{6,22},{7,23},{8,24},{9,... | collective-permute-start | bytes 884744 | tf_op jit(solution)/shard_map/ppermute | solution.py:78
  56.3 14.4 %collective-permute-start.24 = (bf16[2,3,64,384]{3,2,1,0:T(8,128)(2,1)S(1)}, bf16[2,3,64,384]{3,2,1,0:T(8,128)(2,1)S(1)}, u32[]{:S(2)}, u32[]{:S(2)}) collective-permute-start(bf16[2,3,64,384]{3,2,1,0:T(8,128)(2,1)S(1)} %get-tuple-element.102), channel_id=1, source_target_pairs={{0,4},{1,5},{2,6},{3,7},{4,0},{5,1},{6,2},{7,3},{8,12},{9,13},{10,... | collective-permute-start | bytes 884744 | tf_op jit(solution)/shard_map/ppermute | solution.py:78
  71.4 15.5 %collective-permute-start.31 = (bf16[2,3,64,384]{3,2,1,0:T(8,128)(2,1)S(1)}, bf16[2,3,64,384]{3,2,1,0:T(8,128)(2,1)S(1)}, u32[]{:S(2)}, u32[]{:S(2)}) collective-permute-start(bf16[2,3,64,384]{3,2,1,0:T(8,128)(2,1)S(1)} %get-tuple-element.125), channel_id=1, source_target_pairs={{0,8},{1,9},{2,10},{3,11},{4,12},{5,13},{6,14},{7,15},{8,0},{9,1},... | collective-permute-start | bytes 884744 | tf_op jit(solution)/shard_map/ppermute | solution.py:78
  75.3 11.7 %collective-permute-start.27 = (bf16[2,3,64,384]{3,2,1,0:T(8,128)(2,1)S(1)}, bf16[2,3,64,384]{3,2,1,0:T(8,128)(2,1)S(1)}, u32[]{:S(2)}, u32[]{:S(2)}) collective-permute-start(bf16[2,3,64,384]{3,2,1,0:T(8,128)(2,1)S(1)} %get-tuple-element.116), channel_id=1, source_target_pairs={{0,4},{1,5},{2,6},{3,7},{4,0},{5,1},{6,2},{7,3},{8,12},{9,13},{10,... | collective-permute-start | bytes 884744 | tf_op jit(solution)/shard_map/ppermute | solution.py:78
  76.0 17.2 %collective-permute-start.34 = (bf16[2,3,64,384]{3,2,1,0:T(8,128)(2,1)S(1)}, bf16[2,3,64,384]{3,2,1,0:T(8,128)(2,1)S(1)}, u32[]{:S(2)}, u32[]{:S(2)}) collective-permute-start(bf16[2,3,64,384]{3,2,1,0:T(8,128)(2,1)S(1)} %get-tuple-element.131), channel_id=1, source_target_pairs={{0,8},{1,9},{2,10},{3,11},{4,12},{5,13},{6,14},{7,15},{8,0},{9,1},... | collective-permute-start | bytes 884744 | tf_op jit(solution)/shard_map/ppermute | solution.py:78
  78.0 15.3 %collective-permute-start.29 = (bf16[2,32,1024]{2,1,0:T(8,128)(2,1)S(1)}, bf16[2,32,1024]{2,1,0:T(8,128)(2,1)S(1)}, u32[]{:S(2)}, u32[]{:S(2)}) collective-permute-start(bf16[2,32,1024]{2,1,0:T(8,128)(2,1)S(1)} %get-tuple-element.119), channel_id=1, source_target_pairs={{0,16},{1,17},{2,18},{3,19},{4,20},{5,21},{6,22},{7,23},{8,24},{9,... | collective-permute-start | bytes 393224 | tf_op jit(solution)/shard_map/ppermute | solution.py:78
  78.4 15.6 %collective-permute-start.30 = (bf16[2,32,1024]{2,1,0:T(8,128)(2,1)S(1)}, bf16[2,32,1024]{2,1,0:T(8,128)(2,1)S(1)}, u32[]{:S(2)}, u32[]{:S(2)}) collective-permute-start(bf16[2,32,1024]{2,1,0:T(8,128)(2,1)S(1)} %get-tuple-element.120), channel_id=1, source_target_pairs={{0,17},{1,16},{2,19},{3,18},{4,21},{5,20},{6,23},{7,22},{8,25},{9,... | collective-permute-start | bytes 393224 | tf_op jit(solution)/shard_map/ppermute | solution.py:78
  86.9 14.2 %collective-permute-start.32 = (bf16[3,64,384]{2,1,0:T(8,128)(2,1)S(1)}, bf16[3,64,384]{2,1,0:T(8,128)(2,1)S(1)}, u32[]{:S(2)}, u32[]{:S(2)}) collective-permute-start(bf16[3,64,384]{2,1,0:T(8,128)(2,1)S(1)} %get-tuple-element.127), channel_id=1, source_target_pairs={{0,8},{1,9},{2,10},{3,11},{4,12},{5,13},{6,14},{7,15},{8,0},{9,1},... | collective-permute-start | bytes 442376 | tf_op jit(solution)/shard_map/ppermute | solution.py:78
  87.0 14.1 %collective-permute-start.33 = (bf16[3,64,384]{2,1,0:T(8,128)(2,1)S(1)}, bf16[3,64,384]{2,1,0:T(8,128)(2,1)S(1)}, u32[]{:S(2)}, u32[]{:S(2)}) collective-permute-start(bf16[3,64,384]{2,1,0:T(8,128)(2,1)S(1)} %get-tuple-element.128), channel_id=1, source_target_pairs={{0,4},{1,5},{2,6},{3,7},{4,0},{5,1},{6,2},{7,3},{8,12},{9,13},{10,... | collective-permute-start | bytes 442376 | tf_op jit(solution)/shard_map/ppermute | solution.py:78
  93.3 7.9 %collective-permute-start.35 = (bf16[3,64,384]{2,1,0:T(8,128)(2,1)S(1)}, bf16[3,64,384]{2,1,0:T(8,128)(2,1)S(1)}, u32[]{:S(2)}, u32[]{:S(2)}) collective-permute-start(bf16[3,64,384]{2,1,0:T(8,128)(2,1)S(1)} %get-tuple-element.133), channel_id=1, source_target_pairs={{0,8},{1,9},{2,10},{3,11},{4,12},{5,13},{6,14},{7,15},{8,0},{9,1},... | collective-permute-start | bytes 442376 | tf_op jit(solution)/shard_map/ppermute | solution.py:78
  93.4 7.8 %collective-permute-start.36 = (bf16[3,64,384]{2,1,0:T(8,128)(2,1)S(1)}, bf16[3,64,384]{2,1,0:T(8,128)(2,1)S(1)}, u32[]{:S(2)}, u32[]{:S(2)}) collective-permute-start(bf16[3,64,384]{2,1,0:T(8,128)(2,1)S(1)} %get-tuple-element.134), channel_id=1, source_target_pairs={{0,4},{1,5},{2,6},{3,7},{4,0},{5,1},{6,2},{7,3},{8,12},{9,13},{10,... | collective-permute-start | bytes 442376 | tf_op jit(solution)/shard_map/ppermute | solution.py:78
  (19 other events, 75.7 us)
